TPU v7x, 768 devices: a whole 4x8x12 slice. The times are simulated.
768 devices in a mesh: fsdp: 64 (over x, y, core), own: 12 (over z).
Axes of the slice: x: 4, y: 8, z: 12, core: 2. Of those that a mesh axis runs over, the one named last changes fastest.
Arguments:
- grads: bfloat16 [64, 24, 288, 1024], P('fsdp', 'own'), may hold values from -5 to 5
- momentum: float32 [24, 288, 1024], P('own', None, 'fsdp'), may hold values from -6 to 6
- weights: float32 [24, 288, 1024], P('own', None, 'fsdp'), may hold values from -6 to 6
- live_rows: int32 [24], replicated, may hold values from 144 to 288, as said below
Outputs:
- new_momentum: float32 [24, 288, 1024], P('own', None, 'fsdp')
- update: float32 [24, 288, 1024], P('own', None, 'fsdp')
Inputs may be any that keep to these rules, and one draw needn't show every extreme that they name: live_rows[j] is the number of real rows of matrix j; both bounds are reached in every draw.
All inputs are finite; a program needn't handle non-finite values.
Results may differ from a plain program's by a relative error of at most 0.019.
Values may be sent and summed in bfloat16 or wider, within the bound.
No kernel may reach another device: no remote copies, remote signals or barrier semaphores. Data moves between devices by JAX's collectives and lax.ppermute only.
A program may use at most 32 MiB of HBM per device.

v0:
```python
import math

import jax
import jax.numpy as jnp
from jax import lax
from jax.sharding import PartitionSpec as P

ITERS = 5


MOMENTUM_DECAY = 0.95
NORM_EPS = 1e-07
NEWTON_FIRST = 3.4445
NEWTON_SECOND = -4.775
NEWTON_THIRD = 2.0315
UPDATE_SCALE = 0.2
WEIGHT_DECAY = 0.1


def newton_schulz(matrix, iterations):
    for _ in range(iterations):
        gram_block = jnp.dot(matrix, matrix.T, preferred_element_type=jnp.float32).astype(
            jnp.bfloat16
        )
        square = jnp.dot(gram_block, gram_block, preferred_element_type=jnp.float32)
        poly_block = (
            NEWTON_SECOND * gram_block.astype(jnp.float32) + NEWTON_THIRD * square
        ).astype(jnp.bfloat16)
        product = jnp.dot(poly_block, matrix, preferred_element_type=jnp.float32)
        matrix = (NEWTON_FIRST * matrix.astype(jnp.float32) + product).astype(jnp.bfloat16)
    return matrix


def per_device(grads, momentum, weights, live_rows):
    mat_row, height, slab_width = momentum.shape
    n_fsdp = lax.axis_size("fsdp")
    home_index = lax.axis_index("own")
    fsdp_index = lax.axis_index("fsdp")
    nmat = live_rows.shape[0]
    width_all = slab_width * n_fsdp
    slot_ids = jnp.arange(mat_row, dtype=jnp.int32)
    partial_value = grads[0].astype(jnp.float32)
    summed = lax.psum_scatter(partial_value, "fsdp", scatter_dimension=2, tiled=True)
    local_ids = home_index * mat_row + slot_ids
    local_live = jnp.take(live_rows, local_ids)
    row_ids = jnp.arange(height, dtype=jnp.int32)
    row_mask = (row_ids[None, :, None] < local_live[:, None, None]).astype(jnp.float32)
    new_momentum = (MOMENTUM_DECAY * momentum + summed) * row_mask
    everyone = jnp.arange(nmat, dtype=jnp.int32)
    owners = everyone // mat_row
    slots = everyone % mat_row
    held_table = (owners[None, :] == home_index) & (slots[None, :] == slot_ids[:, None])
    held_ids = jnp.sum(jnp.where(held_table, everyone[None, :], 0), axis=1)
    held_live = jnp.take(live_rows, held_ids)
    whole_block = lax.all_gather(new_momentum, "fsdp", axis=2, tiled=True)
    norm_values = jnp.sqrt(jnp.sum(whole_block * whole_block, axis=(1, 2)))
    start_block = (whole_block / (norm_values[:, None, None] + NORM_EPS)).astype(jnp.bfloat16)
    short_rows = height - height // 4

    def short_path(matrix):
        result = newton_schulz(matrix[:short_rows], ITERS)
        filler = jnp.zeros((height - short_rows, width_all), jnp.bfloat16)
        return jnp.concatenate([result, filler], axis=0)

    def full_path(matrix):
        return newton_schulz(matrix, ITERS)

    pieces = []
    for slot_number in range(mat_row):
        result = lax.cond(
            held_live[slot_number] <= short_rows, short_path, full_path, start_block[slot_number]
        )
        pieces.append(lax.dynamic_slice_in_dim(result, fsdp_index * slab_width, slab_width, 1))
    out_slabs = jnp.stack(pieces, axis=0)
    update = (
        UPDATE_SCALE * math.sqrt(width_all) * out_slabs.astype(jnp.float32) + WEIGHT_DECAY * weights
    )
    return (new_momentum, update)


def solution(mesh):
    in_specs = (P("fsdp", "own", None, None), P("own", None, "fsdp"), P("own", None, "fsdp"), P())
    out_specs = (P("own", None, "fsdp"), P("own", None, "fsdp"))
    return jax.shard_map(
        per_device, mesh=mesh, in_specs=in_specs, out_specs=out_specs, check_vma=False
    )
```

profile of v0, /device:TPU:1, one launch (start us, length us, event | category | flops | bytes accessed | tf_op | source)
XLA Modules:
  0.0 296.1 jit_solution(7443426531725109241)
XLA Ops:
  7.2 0.0 copy-start
  7.2 0.0 reduce-scatter.2.cloned.1.call-start
  7.2 1.8 copy.20
  9.0 1.9 bitcast_convert_fusion
  10.9 0.0 copy-start.2
  10.9 0.0 reduce-scatter.2.cloned.1.call-update
  10.9 0.0 all-gather.2.cloned.1.call-start
  11.0 0.1 fusion.184
  11.1 0.0 copy-done
  11.2 0.6 gather_fusion
  11.8 0.1 compare_convert_fusion
  11.9 162.4 %reduce-scatter.2.cloned.1.call-done = f32[2,288,16]{1,2,0:T(8,128)} async-done(((f32[2,288,1024]{1,2,0:T(8,128)}), f32[2,288,16]{1,2,0:T(8,128)}) %reduce-scatter.2.cloned.1.call-update) | async-done | bytes 36880 | tf_op jit(solution)/shard_map/reduce_scatter | solution.py:43
  174.2 0.0 copy-done.2
  174.2 1.4 add_multiply_fusion
  175.7 0.0 all-gather.2.cloned.1.call-update
  175.7 0.6 gather_fusion.1
  176.4 0.6 fusion.186
  178.2 94.1 %all-gather.2.cloned.1.call-done = f32[2,288,1024]{1,2,0:T(8,128)} async-done(((f32[2,288,16]{1,2,0:T(8,128)}), f32[2,288,1024]{1,2,0:T(8,128)}) %all-gather.2.cloned.1.call-update) | async-done | bytes 2359312 | tf_op jit(solution)/shard_map/all_gather | solution.py:55
  272.3 0.0 copy-start.1
  272.3 2.5 multiply_reduce_fusion
  274.8 0.3 copy-done.1
  275.1 0.3 divide_convert_fusion
  275.4 0.2 slice_bitcast_fusion.1
  275.6 6.2 %conditional.2 = (bf16[288,1024]{1,0:T(8,128)(2,1)S(1)}) conditional(s32[]{:T(128)} %bitcast.1, bf16[288,1024]{0,1:T(8,128)(2,1)S(1)} %get-tuple-element.13, bf16[288,1024]{0,1:T(8,128)(2,1)S(1)} %get-tuple-element.13), branch_computations={%region_3.5_spmd, %region_4.6_spmd} | conditional | flops 1945958400 | bytes 12275720 | solution.py:70
  275.6 0.5 convolution_convert_fusion.4
  276.1 0.3 copy.21
  276.4 0.7 fusion
  277.1 0.5 convolution_convert_fusion.3
  277.6 0.7 fusion.1
  278.3 0.5 convolution_convert_fusion.2
  278.8 0.7 fusion.2
  279.5 0.5 convolution_convert_fusion.1
  279.9 0.7 fusion.3
  280.6 0.5 convolution_convert_fusion
  281.1 0.7 fusion.4
  281.8 0.1 constant_dynamic-slice_fusion.1
  281.9 0.1 copy.23
  282.0 0.0 copy-start.3
  282.0 6.4 %conditional.3 = (bf16[288,1024]{1,0:T(8,128)(2,1)S(1)}) conditional(s32[]{:T(128)} %bitcast.4, bf16[288,1024]{0,1:T(8,128)(2,1)S(1)} %get-tuple-element.14, bf16[288,1024]{0,1:T(8,128)(2,1)S(1)} %get-tuple-element.14), branch_computations={%region_5.7_spmd, %region_6.8_spmd} | conditional | flops 1945958400 | bytes 12275720 | solution.py:70
  282.2 0.5 convolution_convert_fusion.14
  282.7 0.3 copy.24
  283.0 0.7 fusion.92
  283.7 0.5 convolution_convert_fusion.13
  284.1 0.7 fusion.93
  284.8 0.5 convolution_convert_fusion.12
  285.3 0.7 fusion.94
  286.0 0.5 convolution_convert_fusion.11
  286.5 0.7 fusion.95
  287.2 0.5 convolution_convert_fusion.10
  287.7 0.7 fusion.96
  288.4 0.1 constant_dynamic-slice_fusion
  288.5 0.1 copy.26
  288.6 0.0 copy-done.3
  288.6 0.6 multiply_add_fusion
  (8 shorter events, 0.1 us)
Async XLA Ops:
  7.2 4.0 %copy-start = (s32[24]{0:T(128)S(1)}, s32[24]{0:T(128)}, u32[]{:S(2)}) copy-start(s32[24]{0:T(128)} %param.13) | copy-start | bytes 292
  7.2 167.1 %reduce-scatter.2.cloned.1.call-start = ((), (), s32[]{:S(2)}) async-start(), calls=%async_computation.1 | async-start | bytes 3194880 | tf_op jit(solution)/shard_map/reduce_scatter | solution.py:43
  10.9 163.4 %copy-start.2 = (f32[2,288,16]{1,2,0:T(8,128)S(1)}, f32[2,288,16]{1,2,0:T(8,128)}, u32[]{:S(2)}) copy-start(f32[2,288,16]{1,2,0:T(8,128)} %param.11) | copy-start | bytes 110596
  10.9 261.3 %all-gather.2.cloned.1.call-start = ((), (), s32[]{:S(2)}) async-start(), calls=%async_computation.2 | async-start | bytes 3194880 | tf_op jit(solution)/shard_map/all_gather | solution.py:55
  272.3 2.8 copy-start.1
  282.0 6.6 %copy-start.3 = (f32[2,288,16]{1,2,0:T(8,128)S(1)}, f32[2,288,16]{1,2,0:T(8,128)}, u32[]{:S(2)}) copy-start(f32[2,288,16]{1,2,0:T(8,128)} %param.12) | copy-start | bytes 110596
Sparse Core Ops, SparseCore 0:
  13.3 160.9 reduce-scatter.1
  178.8 93.4 all-gather.1
where the time goes:
time: 296 us
  waiting for transfers between devices  256 us (86%)
  between operations  15.4 us (5%)
  matrix products  11.7 us (4%)
  other arithmetic  7.06 us (2%)
  local copies, waits for them, and re-layouts  5.04 us (2%)
    reduce_scatter x1, waiting for transfers between devices, per_device(): lax.psum_scatter(partial_value, 'fsdp', scatter_dimension=2, tiled=True)  162 us
    all_gather x1, waiting for transfers between devices, per_device(): whole_block = lax.all_gather(new_momentum, 'fsdp', axis=2, tiled=True)  94.1 us
    dot_general x10, matrix products, newton_schulz(): product = jnp.dot(poly_block, matrix, preferred_element_type=jnp.float32)  6.81 us
  transfers between devices with their start and end apart: 2, of which 2 were waited for; matrix products, arithmetic and copies ran while one was open for 1% of the time, Pallas kernels for 0%

commit v1 on v0

v1 whole, which is shorter than its diff:
```python
import functools
import math

import jax
import jax.numpy as jnp
from jax import lax
from jax.experimental import pallas as pl
from jax.experimental.pallas import tpu as pltpu
from jax.sharding import Mesh, PartitionSpec as P

ITERS = 5
MOMENTUM_DECAY = 0.95
NORM_EPS = 1e-07
NEWTON_FIRST = 3.4445
NEWTON_SECOND = -4.775
NEWTON_THIRD = 2.0315
UPDATE_SCALE = 0.2
WEIGHT_DECAY = 0.1

SMEM = pl.BlockSpec(memory_space=pltpu.SMEM)
VMEM = pl.BlockSpec(memory_space=pltpu.VMEM)
VMEM_LIMIT = 32 * 1024 * 1024
NT = (((1,), (1,)), ((), ()))
NN = (((1,), (0,)), ((), ()))


def mm(a, b, dims):
    return lax.dot_general(a, b, dims, preferred_element_type=jnp.float32)


def pair_sum_kernel(both_ref, out_ref):
    total = both_ref[0].astype(jnp.float32) + both_ref[1].astype(jnp.float32)
    out_ref[...] = total.astype(jnp.bfloat16).T.reshape(out_ref.shape)


def pair_sum(both, chips, cols):
    height, width = both.shape[1:]
    steps = 4
    return pl.pallas_call(
        pair_sum_kernel,
        grid=(steps,),
        in_specs=[pl.BlockSpec((2, height, width // steps), lambda i: (0, 0, i))],
        out_specs=pl.BlockSpec((chips // steps, cols, height), lambda i: (i, 0, 0)),
        out_shape=jax.ShapeDtypeStruct((chips, cols, height), jnp.bfloat16),
        compiler_params=pltpu.CompilerParams(vmem_limit_bytes=VMEM_LIMIT),
    )(both)


def momentum_kernel(place_ref, live_ref, parts_ref, old_ref, new_ref, copies_ref):
    chips = parts_ref.shape[0]
    summed = parts_ref[0].astype(jnp.float32)
    for k in range(1, chips):
        summed = summed + parts_ref[k].astype(jnp.float32)
    rows = lax.broadcasted_iota(jnp.int32, summed.shape, 1)
    live = live_ref[place_ref[0]]
    new = jnp.where(rows < live, MOMENTUM_DECAY * old_ref[...] + summed, 0.0)
    new_ref[...] = new
    rounded = new.astype(jnp.bfloat16)
    for k in range(chips):
        copies_ref[k] = rounded


def momentum_step(place, live_rows, parts, old):
    return pl.pallas_call(
        momentum_kernel,
        in_specs=[SMEM, SMEM, VMEM, VMEM],
        out_specs=[VMEM, VMEM],
        out_shape=[
            jax.ShapeDtypeStruct(old.shape, jnp.float32),
            jax.ShapeDtypeStruct(parts.shape, jnp.bfloat16),
        ],
        compiler_params=pltpu.CompilerParams(vmem_limit_bytes=VMEM_LIMIT),
    )(place, live_rows, parts, old)


def newton_kernel(place_ref, gathered_ref, out_ref):
    chips, cols, height = gathered_ref.shape
    width = chips * cols
    x = gathered_ref[...].reshape(width, height).T
    raw = mm(x, x, NT)
    row = lax.broadcasted_iota(jnp.int32, (height, height), 0)
    col = lax.broadcasted_iota(jnp.int32, (height, height), 1)
    norm = jnp.sqrt(jnp.sum(jnp.where(row == col, raw, 0.0), keepdims=True))
    scale = 1.0 / (norm + NORM_EPS)
    gram = (raw * scale * scale).astype(jnp.bfloat16)
    for step in range(ITERS):
        if step:
            gram = mm(x, x, NT).astype(jnp.bfloat16)
        square = mm(gram, gram, NN)
        poly = (NEWTON_SECOND * gram.astype(jnp.float32) + NEWTON_THIRD * square).astype(jnp.bfloat16)
        if step == ITERS - 1:
            place = place_ref[1] * cols
            want = lax.broadcasted_iota(jnp.int32, (cols, width), 0) + place
            have = lax.broadcasted_iota(jnp.int32, (cols, width), 1)
            pick = (want == have).astype(jnp.bfloat16)
            mine = mm(pick, x, NT)
            out_ref[...] = NEWTON_FIRST * mine + mm(mine.astype(jnp.bfloat16), poly, NT)
        else:
            x = NEWTON_FIRST * x.astype(jnp.float32) + mm(poly, x, NN)
            if step == 0:
                x = x * scale
            x = x.astype(jnp.bfloat16)


def newton(place, gathered):
    return pl.pallas_call(
        newton_kernel,
        in_specs=[SMEM, VMEM],
        out_specs=VMEM,
        out_shape=jax.ShapeDtypeStruct(gathered.shape[1:], jnp.float32),
        compiler_params=pltpu.CompilerParams(vmem_limit_bytes=VMEM_LIMIT),
    )(place, gathered)


def per_device(grads, momentum, weights, live_rows):
    cores = lax.axis_size("core")
    chips = lax.axis_size("x") * lax.axis_size("y")
    slab = momentum.shape[2]
    height = momentum.shape[1]
    cols = cores * slab
    width = chips * cols
    chip = lax.axis_index("x") * lax.axis_size("y") + lax.axis_index("y")
    matrix = lax.axis_index("own") * cores + lax.axis_index("core")
    place = jnp.stack([matrix, chip]).astype(jnp.int32)
    both = lax.all_to_all(grads[0], "core", 0, 0)
    old = lax.all_to_all(jnp.swapaxes(momentum, 1, 2), "core", 0, 0)
    parts = pair_sum(both, chips, cols)
    parts = lax.all_to_all(parts, ("x", "y"), 0, 0)
    new, copies = momentum_step(place, live_rows, parts, old.reshape(cols, height))
    gathered = lax.all_to_all(copies, ("x", "y"), 0, 0)
    ortho = newton(place, gathered)
    back = jnp.stack([new.reshape(cores, slab, height), ortho.reshape(cores, slab, height)], axis=1)
    back = lax.all_to_all(back, "core", 0, 0)
    new_momentum = jnp.swapaxes(back[:, 0], 1, 2)
    update = UPDATE_SCALE * math.sqrt(width) * jnp.swapaxes(back[:, 1], 1, 2) + WEIGHT_DECAY * weights
    return (new_momentum, update)


def solution(mesh):
    fsdp, own = mesh.devices.shape
    assert (fsdp, own) == (64, 12)
    split = Mesh(mesh.devices.reshape(4, 8, 2, own), ("x", "y", "core", "own"))
    all_fsdp = ("x", "y", "core")
    in_specs = (P(all_fsdp, "own", None, None), P("own", None, all_fsdp), P("own", None, all_fsdp), P())
    out_specs = (P("own", None, all_fsdp), P("own", None, all_fsdp))
    return jax.shard_map(
        per_device, mesh=split, in_specs=in_specs, out_specs=out_specs, check_vma=False
    )
```

time: 296 us -> 90.1 us (0.30)
  waiting for transfers between devices: 256 us -> 21.5 us
  blocking collectives: 0 us -> 50.2 us
  between operations: 15.4 us -> 0.69 us
  matrix products: 11.7 us -> 0 us
  Pallas kernels: 0 us -> 8.24 us
  starting transfers between devices: 0.08 us -> 7.68 us
  other arithmetic: 7.06 us -> 0.72 us
  local copies, waits for them, and re-layouts: 5.04 us -> 0.63 us
    reduce_scatter x1 -> x0, waiting for transfers between devices: 162 us -> none  [per_device(): lax.psum_scatter(partial_value, 'fsdp', scatter_dimension=2, tiled=True)]
    all_gather x1 -> x0, waiting for transfers between devices: 94.1 us -> none  [per_device(): whole_block = lax.all_gather(new_momentum, 'fsdp', axis=2, tiled=True)]
    all_to_all x0 -> x3, blocking collectives: none -> 50.2 us  [the longest x1 25.7 us: per_device(): gathered = lax.all_to_all(copies, ('x', 'y'), 0, 0)]
    all_to_all x0 -> x2, waiting for transfers between devices: none -> 21.5 us  [the longest x1 21.5 us: per_device(): parts = lax.all_to_all(parts, ('x', 'y'), 0, 0)]
    dot_general x20 -> x0, matrix products: 11.7 us -> none  [the longest x10 6.81 us: newton_schulz(): product = jnp.dot(poly_block, matrix, preferred_element_type=jnp.float32)]
    pallas_call x0 -> x3, Pallas kernels: none -> 8.24 us  [the longest x1 5.71 us: newton(): pl.pallas_call(newton_kernel, in_specs=[SMEM, VMEM], out_specs=VMEM, out_...]
    all_to_all x0 -> x2, starting transfers between devices: none -> 7.68 us  [the longest x1 4.04 us: per_device(): parts = lax.all_to_all(parts, ('x', 'y'), 0, 0)]
  transfers between devices with their start and end apart: 2 -> 2, of which waited for: 2 -> 1; matrix products, arithmetic and copies ran while one was open for 1% -> 0% of each run, Pallas kernels for 0% -> 2%
where the time goes in v1:
time: 90.1 us; the launch traced here: 89.6 us
  blocking collectives  50.2 us (56%)
  waiting for transfers between devices  21.5 us (24%)
  Pallas kernels  8.24 us (9%)
  starting transfers between devices  7.68 us (9%)
    all_to_all x1, blocking collectives, per_device(): gathered = lax.all_to_all(copies, ('x', 'y'), 0, 0)  25.7 us
    all_to_all x1, waiting for transfers between devices, per_device(): parts = lax.all_to_all(parts, ('x', 'y'), 0, 0)  21.5 us
    all_to_all x1, blocking collectives, per_device(): both = lax.all_to_all(grads[0], 'core', 0, 0)  16 us
    all_to_all x1, blocking collectives, per_device(): back = lax.all_to_all(back, 'core', 0, 0)  8.56 us
    pallas_call x1, Pallas kernels, newton(): pl.pallas_call(newton_kernel, in_specs=[SMEM, VMEM], out_specs=VMEM, out_...  5.71 us
    all_to_all x1, starting transfers between devices, per_device(): parts = lax.all_to_all(parts, ('x', 'y'), 0, 0)  4.04 us
    all_to_all x1, starting transfers between devices, per_device(): old = lax.all_to_all(jnp.swapaxes(momentum, 1, 2), 'core', 0, 0)  3.64 us
    pallas_call x1, Pallas kernels, pair_sum(): pl.pallas_call(pair_sum_kernel, grid=(steps,), in_specs=[pl.BlockSpec((2,...  1.84 us
  transfers between devices with their start and end apart: 2, of which 1 were waited for; matrix products, arithmetic and copies ran while one was open for 0% of the time, Pallas kernels for 2%

profile of v1, /device:TPU:1, one launch (start us, length us, event | category | flops | bytes accessed | tf_op | source)
XLA Modules:
  0.0 89.6 jit_solution(15767748818712169358)
XLA Ops:
  0.6 16.0 %all_to_all.25.both_ref = bf16[2,288,1024]{2,1,0:T(8,128)(2,1)S(1)} all-to-all(bf16[2,288,1024]{2,1,0:T(8,128)(2,1)} %bitcast.24), channel_id=1, replica_groups=mesh['x'=4,'y'=8,'core'=2,'own'=12] {'core'}, dimensions={0} | all-to-all | bytes 2359296 | tf_op jit(solution)/shard_map/all_to_all | solution.py:125
  16.6 3.6 %all-to-all-start.2 = ((f32[2,16,288]{2,1,0:T(8,128)}), f32[2,16,288]{2,1,0:T(8,128)S(1)}, u32[]{:S(2)}, u32[]{:S(2)}) async-start(f32[2,16,288]{2,1,0:T(8,128)} %bitcast.3), calls=%async_computation.2 | async-start | bytes 98304 | tf_op jit(solution)/shard_map/all_to_all | solution.py:126
  20.2 1.8 %shard_map.59 = bf16[32,32,288]{2,1,0:T(8,128)(2,1)} custom-call(bf16[2,288,1024]{2,1,0:T(8,128)(2,1)S(1)} %all_to_all.25.both_ref), custom_call_target="tpu_custom_call" | custom-call | tf_op jit(solution)/shard_map/pallas_call | solution.py:39
  22.1 0.0 copy-start
  22.1 0.0 all-to-all-done.2
  22.1 4.0 %all-to-all-start.1 = ((bf16[32,32,288]{2,1,0:T(8,128)(2,1)}), bf16[32,32,288]{2,1,0:T(8,128)(2,1)S(1)}, u32[]{:S(2)}, u32[]{:S(2)}) async-start(bf16[32,32,288]{2,1,0:T(8,128)(2,1)} %shard_map.59), calls=%async_computation.1 | async-start | bytes 1572864 | tf_op jit(solution)/shard_map/all_to_all | solution.py:128
  26.1 0.1 pad_add_fusion.place_ref
  26.2 21.5 %all-to-all-done.1.parts_ref = bf16[32,32,288]{2,1,0:T(8,128)(2,1)S(1)} async-done(((bf16[32,32,288]{2,1,0:T(8,128)(2,1)}), bf16[32,32,288]{2,1,0:T(8,128)(2,1)S(1)}, u32[]{:S(2)}, u32[]{:S(2)}) %all-to-all-start.1) | async-done | bytes 589856 | tf_op jit(solution)/shard_map/all_to_all | solution.py:128
  47.7 0.0 copy-done
  47.7 0.7 shard_map.60
  48.4 0.0 copy-start.1
  48.4 25.7 %all_to_all.26.gathered_ref = bf16[32,32,288]{2,1,0:T(8,128)(2,1)S(1)} all-to-all(bf16[32,32,288]{2,1,0:T(8,128)(2,1)S(1)} %get-tuple-element.5), channel_id=1, replica_groups=mesh['x'=4,'y'=8,'core'=2,'own'=12] {'x','y'}, dimensions={0} | all-to-all | bytes 1179648 | tf_op jit(solution)/shard_map/all_to_all | solution.py:130
  74.1 5.7 %shard_map.61 = f32[32,288]{1,0:T(8,128)S(1)} custom-call(s32[2]{0:T(128)S(1)} %pad_add_fusion.place_ref, bf16[32,32,288]{2,1,0:T(8,128)(2,1)S(1)} %all_to_all.26.gathered_ref), custom_call_target="tpu_custom_call" | custom-call | tf_op jit(solution)/shard_map/pallas_call | solution.py:106
  79.8 8.6 %all_to_all.27 = f32[2,2,16,288]{3,2,1,0:T(8,128)S(1)} all-to-all(f32[2,2,16,288]{3,2,1,0:T(8,128)S(1)} %pad_maximum_fusion), channel_id=1, replica_groups=mesh['x'=4,'y'=8,'core'=2,'own'=12] {'core'}, dimensions={0} | all-to-all | bytes 147456 | tf_op jit(solution)/shard_map/all_to_all | solution.py:133
  88.4 0.6 slice_bitcast_fusion
  89.0 0.0 copy-done.1
  89.0 0.6 fusion.1
  (1 shorter events, 0.0 us)
Async XLA Ops:
  16.6 5.5 %all-to-all-start.2 = ((f32[2,16,288]{2,1,0:T(8,128)}), f32[2,16,288]{2,1,0:T(8,128)S(1)}, u32[]{:S(2)}, u32[]{:S(2)}) async-start(f32[2,16,288]{2,1,0:T(8,128)} %bitcast.3), calls=%async_computation.2 | async-start | bytes 98304 | tf_op jit(solution)/shard_map/all_to_all | solution.py:126
  22.1 25.6 %copy-start = (s32[24]{0:T(128)S(1)}, s32[24]{0:T(128)}, u32[]{:S(2)}) copy-start(s32[24]{0:T(128)} %live_ref.1) | copy-start | bytes 292
  22.1 25.6 %all-to-all-start.1 = ((bf16[32,32,288]{2,1,0:T(8,128)(2,1)}), bf16[32,32,288]{2,1,0:T(8,128)(2,1)S(1)}, u32[]{:S(2)}, u32[]{:S(2)}) async-start(bf16[32,32,288]{2,1,0:T(8,128)(2,1)} %shard_map.59), calls=%async_computation.1 | async-start | bytes 1572864 | tf_op jit(solution)/shard_map/all_to_all | solution.py:128
  48.4 40.6 %copy-start.1 = (f32[2,288,16]{1,2,0:T(8,128)S(1)}, f32[2,288,16]{1,2,0:T(8,128)}, u32[]{:S(2)}) copy-start(f32[2,288,16]{1,2,0:T(8,128)} %param.6) | copy-start | bytes 110596

commit v2 on v1

v2 whole, which is shorter than its diff:
```python
import math

import jax
import jax.numpy as jnp
from jax import lax
from jax.experimental import pallas as pl
from jax.experimental.pallas import tpu as pltpu
from jax.sharding import Mesh, PartitionSpec as P

ITERS = 5
MOMENTUM_DECAY = 0.95
NORM_EPS = 1e-07
NEWTON_FIRST = 3.4445
NEWTON_SECOND = -4.775
NEWTON_THIRD = 2.0315
UPDATE_SCALE = 0.2
WEIGHT_DECAY = 0.1

LANES = 128
SMEM = pl.BlockSpec(memory_space=pltpu.SMEM)
VMEM = pl.BlockSpec(memory_space=pltpu.VMEM)
PARAMS = pltpu.CompilerParams(vmem_limit_bytes=32 * 1024 * 1024)
NT = (((1,), (1,)), ((), ()))
NN = (((1,), (0,)), ((), ()))
TN = (((0,), (0,)), ((), ()))

CORE, CHIP, MATRIX = 0, 1, 2


def mm(a, b, dims, precision=None):
    return lax.dot_general(a, b, dims, precision=precision, preferred_element_type=jnp.float32)


def pair_sum_kernel(place_ref, own_ref, other_ref, old_ref, out_ref):
    step = pl.program_id(0)
    chunks = out_ref.shape[0]
    total = own_ref[0].astype(jnp.float32) + other_ref[...].astype(jnp.float32)
    for q in range(chunks):
        out_ref[q] = total[:, q * LANES:(q + 1) * LANES].astype(jnp.bfloat16)
    cores, _, slab, height = old_ref.shape
    cols = cores * slab
    per_chunk = LANES // cols
    chip = place_ref[CHIP]

    @pl.when(chip // per_chunk // chunks == step)
    def _():
        old = MOMENTUM_DECAY * old_ref[:, 0].reshape(cols, height)
        want = lax.broadcasted_iota(jnp.int32, (cols, LANES), 0) + (chip % per_chunk) * cols
        have = lax.broadcasted_iota(jnp.int32, (cols, LANES), 1)
        spread = mm(old, (want == have).astype(jnp.float32), TN, lax.Precision.HIGHEST)
        for q in range(chunks):

            @pl.when(chip // per_chunk % chunks == q)
            def _():
                mine = total[:, q * LANES:(q + 1) * LANES] + spread
                out_ref[q] = mine.astype(jnp.bfloat16)


def pair_sum(place, own, other, old):
    height, width = other.shape
    cores, _, slab, _ = old.shape
    steps = 2
    chunks = width // LANES // steps
    return pl.pallas_call(
        pair_sum_kernel,
        grid_spec=pltpu.PrefetchScalarGridSpec(
            num_scalar_prefetch=1,
            grid=(steps,),
            in_specs=[
                pl.BlockSpec((1, height, chunks * LANES), lambda i, place: (place[CORE], 0, i)),
                pl.BlockSpec((height, chunks * LANES), lambda i, place: (0, i)),
                pl.BlockSpec((cores, 1, slab, height), lambda i, place: (0, place[CORE], 0, 0)),
            ],
            out_specs=pl.BlockSpec((chunks, height, LANES), lambda i, place: (i, 0, 0)),
        ),
        out_shape=jax.ShapeDtypeStruct((width // LANES, height, LANES), jnp.bfloat16),
        compiler_params=PARAMS,
    )(place, own, other, old)


def add_parts(parts_ref):
    total = parts_ref[0].astype(jnp.float32)
    for k in range(1, parts_ref.shape[0]):
        total = total + parts_ref[k].astype(jnp.float32)
    return total


def sum_kernel(parts_ref, copies_ref):
    total = add_parts(parts_ref).astype(jnp.bfloat16)
    for k in range(copies_ref.shape[0]):
        copies_ref[k] = total


def sum_and_copy(parts, copies):
    return pl.pallas_call(
        sum_kernel,
        in_specs=[VMEM],
        out_specs=VMEM,
        out_shape=jax.ShapeDtypeStruct((copies,) + parts.shape[1:], jnp.bfloat16),
        compiler_params=PARAMS,
    )(parts)


def mask_kernel(place_ref, live_ref, parts_ref, copies_ref):
    total = add_parts(parts_ref)
    rows = lax.broadcasted_iota(jnp.int32, total.shape, 0)
    live = live_ref[place_ref[MATRIX]]
    new = jnp.where(rows < live, total, 0.0).astype(jnp.bfloat16)
    for k in range(copies_ref.shape[0]):
        copies_ref[k] = new


def sum_mask_and_copy(place, live_rows, parts, copies):
    return pl.pallas_call(
        mask_kernel,
        in_specs=[SMEM, SMEM, VMEM],
        out_specs=VMEM,
        out_shape=jax.ShapeDtypeStruct((copies,) + parts.shape[1:], jnp.bfloat16),
        compiler_params=PARAMS,
    )(place, live_rows, parts)


def newton_kernel(place_ref, gathered_ref, out_ref):
    chunks, height, _ = gathered_ref.shape
    cols = out_ref.shape[1]
    width = chunks * LANES
    x = jnp.concatenate([gathered_ref[q] for q in range(chunks)], axis=1)
    want = lax.broadcasted_iota(jnp.int32, (cols, width), 0) + place_ref[CHIP] * cols
    have = lax.broadcasted_iota(jnp.int32, (cols, width), 1)
    pick = (want == have).astype(jnp.bfloat16)
    out_ref[0] = mm(pick, x, NT)
    raw = mm(x, x, NT)
    row = lax.broadcasted_iota(jnp.int32, (height, height), 0)
    col = lax.broadcasted_iota(jnp.int32, (height, height), 1)
    norm = jnp.sqrt(jnp.sum(jnp.where(row == col, raw, 0.0), keepdims=True))
    scale = 1.0 / (norm + NORM_EPS)
    gram = (raw * scale * scale).astype(jnp.bfloat16)
    for step in range(ITERS):
        if step:
            gram = mm(x, x, NT).astype(jnp.bfloat16)
        square = mm(gram, gram, NN)
        poly = (NEWTON_SECOND * gram.astype(jnp.float32) + NEWTON_THIRD * square).astype(jnp.bfloat16)
        if step == ITERS - 1:
            mine = mm(pick, x, NT)
            out_ref[1] = NEWTON_FIRST * mine + mm(mine.astype(jnp.bfloat16), poly, NT)
        else:
            x = NEWTON_FIRST * x.astype(jnp.float32) + mm(poly, x, NN)
            if step == 0:
                x = x * scale
            x = x.astype(jnp.bfloat16)


def newton(place, gathered, cols):
    return pl.pallas_call(
        newton_kernel,
        in_specs=[SMEM, VMEM],
        out_specs=VMEM,
        out_shape=jax.ShapeDtypeStruct((2, cols, gathered.shape[1]), jnp.float32),
        compiler_params=PARAMS,
    )(place, gathered)


def finish_kernel(factor, place_ref, back_ref, weights_ref, new_ref, update_ref):
    mats, slab, _ = weights_ref.shape
    mine = pl.ds(pl.multiple_of(place_ref[CORE] * slab, slab), slab)
    for m in range(mats):
        new_ref[m] = back_ref[m, 0, mine, :]
        update_ref[m] = factor * back_ref[m, 1, mine, :] + WEIGHT_DECAY * weights_ref[m]


def finish(place, back, weights, factor):
    def kernel(*refs):
        finish_kernel(factor, *refs)

    shape = jax.ShapeDtypeStruct(weights.shape, jnp.float32)
    return pl.pallas_call(
        kernel,
        in_specs=[SMEM, VMEM, VMEM],
        out_specs=[VMEM, VMEM],
        out_shape=[shape, shape],
        compiler_params=PARAMS,
    )(place, back, weights)


def per_device(grads, momentum, weights, live_rows):
    mats, height, slab = momentum.shape
    cores = lax.axis_size("core")
    y_low, y_high = lax.axis_size("y_low"), lax.axis_size("y_high")
    width = grads.shape[3]
    core = lax.axis_index("core")
    chip = (lax.axis_index("x") * y_high + lax.axis_index("y_high")) * y_low + lax.axis_index("y_low")
    matrix = lax.axis_index("own") * mats + core
    place = jnp.stack([core, chip, matrix]).astype(jnp.int32)
    group = ("x", "y_low")
    given = lax.dynamic_index_in_dim(grads[0], cores - 1 - core, 0, keepdims=False)
    other = lax.ppermute(given, "core", [(0, 1), (1, 0)])
    old = lax.all_gather(jnp.swapaxes(momentum, 1, 2), "core")
    chunks = pair_sum(place, grads[0], other, old)
    chunks = lax.all_to_all(chunks, group, 0, 0)
    chunk = sum_and_copy(chunks, y_high)
    chunk = lax.all_to_all(chunk, "y_high", 0, 0)
    copies = sum_mask_and_copy(place, live_rows, chunk, width // LANES)
    gathered = lax.all_to_all(copies, group, 0, 0)
    mine = newton(place, gathered, cores * slab)
    back = lax.all_gather(mine, "core")
    new_momentum, update = finish(
        place, back, jnp.swapaxes(weights, 1, 2), UPDATE_SCALE * math.sqrt(width)
    )
    return (jnp.swapaxes(new_momentum, 1, 2), jnp.swapaxes(update, 1, 2))


def solution(mesh):
    fsdp, own = mesh.devices.shape
    assert (fsdp, own) == (64, 12)
    split = Mesh(mesh.devices.reshape(4, 4, 2, 2, own), ("x", "y_high", "y_low", "core", "own"))
    all_fsdp = ("x", "y_high", "y_low", "core")
    in_specs = (P(all_fsdp, "own", None, None), P("own", None, all_fsdp), P("own", None, all_fsdp), P())
    out_specs = (P("own", None, all_fsdp), P("own", None, all_fsdp))
    return jax.shard_map(
        per_device, mesh=split, in_specs=in_specs, out_specs=out_specs, check_vma=False
    )
```

time: 90.1 us -> 68.1 us (0.76)
  waiting for transfers between devices: 21.5 us -> 0.01 us
  blocking collectives: 50.2 us -> 44.3 us
  starting transfers between devices: 7.68 us -> 12.4 us
    all_to_all x2 -> x0, waiting for transfers between devices: 21.5 us -> none  [the longest x1 21.5 us: per_device(): parts = lax.all_to_all(parts, ('x', 'y'), 0, 0)]
    all_to_all x3, blocking collectives: 50.2 us -> 37.4 us  [the longest x1 13.2 us: per_device(): chunks = lax.all_to_all(chunks, group, 0, 0)]
    ppermute x0 -> x1, starting transfers between devices: none -> 12.4 us  [per_device(): other = lax.ppermute(given, 'core', [(0, 1), (1, 0)])]
    all_to_all x2 -> x0, starting transfers between devices: 7.68 us -> none  [the longest x1 4.04 us: per_device(): parts = lax.all_to_all(parts, ('x', 'y'), 0, 0)]
    all_gather x0 -> x2, blocking collectives: none -> 6.89 us  [the longest x1 5.01 us: per_device(): back = lax.all_gather(mine, 'core')]
    squeeze x0 -> x1, local copies, waits for them, and re-layouts: none -> 1.2 us  [per_device(): lax.dynamic_index_in_dim(grads[0], cores - 1 - core, 0, keepdims=False)]
    pallas_call x2 -> x4, Pallas kernels: 2.53 us -> 3.1 us  [the longest x1 1.23 us: pair_sum(): pl.pallas_call(pair_sum_kernel, grid_spec=pltpu.PrefetchScalarGridSpec(nu...]
  transfers between devices with their start and end apart: 2 -> 1, of which waited for: 1 -> 0; matrix products, arithmetic and copies ran while one was open for 0% -> 0% of each run, Pallas kernels for 2% -> 0%
where the time goes in v2:
time: 68.1 us; the launch traced here: 67.8 us
  blocking collectives  44.3 us (65%)
  starting transfers between devices  12.4 us (18%)
  Pallas kernels  8.97 us (13%)
  local copies, waits for them, and re-layouts  1.22 us (2%)
  between operations  0.74 us (1%)
    all_to_all x1, blocking collectives, per_device(): chunks = lax.all_to_all(chunks, group, 0, 0)  13.2 us
    all_to_all x1, blocking collectives, per_device(): gathered = lax.all_to_all(copies, group, 0, 0)  12.6 us
    ppermute x1, starting transfers between devices, per_device(): other = lax.ppermute(given, 'core', [(0, 1), (1, 0)])  12.4 us
    all_to_all x1, blocking collectives, per_device(): chunk = lax.all_to_all(chunk, 'y_high', 0, 0)  11.6 us
    pallas_call x1, Pallas kernels, newton(): pl.pallas_call(newton_kernel, in_specs=[SMEM, VMEM], out_specs=VMEM, out_...  5.87 us
    all_gather x1, blocking collectives, per_device(): back = lax.all_gather(mine, 'core')  5.01 us
    all_gather x1, blocking collectives, per_device(): old = lax.all_gather(jnp.swapaxes(momentum, 1, 2), 'core')  1.88 us
  transfers between devices with their start and end apart: 1, of which 0 were waited for; matrix products, arithmetic and copies ran while one was open for 0% of the time, Pallas kernels for 0%

profile of v2, /device:TPU:1, one launch (start us, length us, event | category | flops | bytes accessed | tf_op | source)
XLA Modules:
  0.0 67.8 jit_solution(17852513257028778910)
XLA Ops:
  0.6 0.0 copy-start
  0.6 0.0 copy-start.3
  0.7 1.2 %dynamic-slice_bitcast_fusion = bf16[288,1024]{1,0:T(8,128)(2,1)S(1)} fusion(bf16[1,2,288,1024]{3,2,1,0:T(8,128)(2,1)} %param.4, s32[]{:T(128)S(6)} %select_n.4), kind=kLoop, calls=%fused_computation | loop fusion | bytes 1179652 | tf_op jit(solution)/shard_map/jit(dynamic_index_in_dim)/squeeze | solution.py:195
  1.9 12.4 %collective-permute-start = (bf16[288,1024]{1,0:T(8,128)(2,1)S(1)}, bf16[288,1024]{1,0:T(8,128)(2,1)S(1)}, u32[]{:S(2)}, u32[]{:S(2)}) collective-permute-start(bf16[288,1024]{1,0:T(8,128)(2,1)S(1)} %dynamic-slice_bitcast_fusion), channel_id=1, source_target_pairs={{0,12},{12,0},{1,13},{13,1},{2,14},{14,2},{3,15},{15,3},{4,16},{16... | collective-permute-start | bytes 1769480 | tf_op jit(solution)/shard_map/ppermute | solution.py:196
  14.3 0.0 copy-done.3
  14.3 1.9 %all-gather = f32[4,16,288]{2,1,0:T(8,128)S(1)} all-gather(f32[2,16,288]{2,1,0:T(8,128)S(1)} %bitcast.16), channel_id=2, replica_groups=mesh['x'=4,'y_high'=4,'y_low'=2,'core'=2,'own'=12] {'core'}, dimensions={0}, use_global_device_ids=true | all-gather | bytes 110592 | tf_op jit(solution)/shard_map/all_gather | solution.py:197
  16.2 0.1 pad_add_fusion.place_ref.refs_0_
  16.3 0.0 collective-permute-done.other_ref
  16.3 0.0 copy-done
  16.3 1.2 %shard_map.59 = bf16[8,288,128]{2,1,0:T(8,128)(2,1)S(1)} custom-call(s32[3]{0:T(128)S(1)} %pad_add_fusion.place_ref.refs_0_, bf16[2,288,1024]{2,1,0:T(8,128)(2,1)S(1)} %bitcast.12, bf16[288,1024]{1,0:T(8,128)(2,1)S(1)} %collective-permute-done.other_ref, f32[2,2,16,288]{3,2,1,0:T(8,128)S(1)} %bitcast.14), custom_call_target="tpu_custom_call" | custom-call | tf_op jit(solution)/shard_map/pallas_call | solution.py:64
  17.5 0.0 copy-start.2
  17.5 13.2 %all_to_all.15.parts_ref = bf16[8,288,128]{2,1,0:T(8,128)(2,1)S(1)} all-to-all(bf16[8,288,128]{2,1,0:T(8,128)(2,1)S(1)} %shard_map.59), channel_id=1, replica_groups=mesh['x'=4,'y_high'=4,'y_low'=2,'core'=2,'own'=12] {'x','y_low'}, dimensions={0} | all-to-all | bytes 1179648 | tf_op jit(solution)/shard_map/all_to_all | solution.py:199
  30.7 0.1 shard_map.60
  30.8 11.6 %all_to_all.16.parts_ref = bf16[4,288,128]{2,1,0:T(8,128)(2,1)S(1)} all-to-all(bf16[4,288,128]{2,1,0:T(8,128)(2,1)S(1)} %shard_map.60), channel_id=1, replica_groups=mesh['x'=4,'y_high'=4,'y_low'=2,'core'=2,'own'=12] {'y_high'}, dimensions={0} | all-to-all | bytes 589824 | tf_op jit(solution)/shard_map/all_to_all | solution.py:201
  42.4 0.0 copy-done.2
  42.4 0.6 shard_map.61
  43.0 0.0 copy-start.1
  43.0 12.6 %all_to_all.17.gathered_ref = bf16[8,288,128]{2,1,0:T(8,128)(2,1)S(1)} all-to-all(bf16[8,288,128]{2,1,0:T(8,128)(2,1)S(1)} %shard_map.61), channel_id=1, replica_groups=mesh['x'=4,'y_high'=4,'y_low'=2,'core'=2,'own'=12] {'x','y_low'}, dimensions={0} | all-to-all | bytes 1179648 | tf_op jit(solution)/shard_map/all_to_all | solution.py:203
  55.7 5.9 %shard_map.62 = f32[2,32,288]{2,1,0:T(8,128)S(1)} custom-call(s32[3]{0:T(128)S(1)} %pad_add_fusion.place_ref.refs_0_, bf16[8,288,128]{2,1,0:T(8,128)(2,1)S(1)} %all_to_all.17.gathered_ref), custom_call_target="tpu_custom_call" | custom-call | tf_op jit(solution)/shard_map/pallas_call | solution.py:154
  61.6 5.0 %all-gather.1 = f32[4,32,288]{2,1,0:T(8,128)S(1)} all-gather(f32[2,32,288]{2,1,0:T(8,128)S(1)} %shard_map.62), channel_id=3, replica_groups=mesh['x'=4,'y_high'=4,'y_low'=2,'core'=2,'own'=12] {'core'}, dimensions={0}, use_global_device_ids=true | all-gather | bytes 221184 | tf_op jit(solution)/shard_map/all_gather | solution.py:205
  66.6 0.0 copy-done.1
  66.6 1.2 %shard_map.63 = (f32[2,16,288]{2,1,0:T(8,128)}, f32[2,16,288]{2,1,0:T(8,128)}) custom-call(s32[3]{0:T(128)S(1)} %pad_add_fusion.place_ref.refs_0_, f32[2,2,32,288]{3,2,1,0:T(8,128)S(1)} %bitcast.13, f32[2,16,288]{2,1,0:T(8,128)S(1)} %bitcast.15), custom_call_target="tpu_custom_call" | custom-call | tf_op jit(solution)/shard_map/pallas_call | solution.py:176
Async XLA Ops:
  0.6 15.7 %copy-start = (bf16[1,2,288,1024]{3,2,1,0:T(8,128)(2,1)S(1)}, bf16[1,2,288,1024]{3,2,1,0:T(8,128)(2,1)}, u32[]{:S(2)}) copy-start(bf16[1,2,288,1024]{3,2,1,0:T(8,128)(2,1)} %param.4) | copy-start | bytes 3538948
  0.6 13.7 %copy-start.3 = (f32[2,288,16]{1,2,0:T(8,128)S(1)}, f32[2,288,16]{1,2,0:T(8,128)}, u32[]{:S(2)}) copy-start(f32[2,288,16]{1,2,0:T(8,128)} %param.5) | copy-start | bytes 110596
  1.9 14.4 %collective-permute-start = (bf16[288,1024]{1,0:T(8,128)(2,1)S(1)}, bf16[288,1024]{1,0:T(8,128)(2,1)S(1)}, u32[]{:S(2)}, u32[]{:S(2)}) collective-permute-start(bf16[288,1024]{1,0:T(8,128)(2,1)S(1)} %dynamic-slice_bitcast_fusion), channel_id=1, source_target_pairs={{0,12},{12,0},{1,13},{13,1},{2,14},{14,2},{3,15},{15,3},{4,16},{16... | collective-permute-start | bytes 1769480 | tf_op jit(solution)/shard_map/ppermute | solution.py:196
  17.5 24.9 %copy-start.2 = (s32[24]{0:T(128)S(1)}, s32[24]{0:T(128)}, u32[]{:S(2)}) copy-start(s32[24]{0:T(128)} %live_ref.1) | copy-start | bytes 292
  43.0 23.5 %copy-start.1 = (f32[2,288,16]{1,2,0:T(8,128)S(1)}, f32[2,288,16]{1,2,0:T(8,128)}, u32[]{:S(2)}) copy-start(f32[2,288,16]{1,2,0:T(8,128)} %param.6) | copy-start | bytes 110596

commit v3 on v2

v3 whole, which is shorter than its diff:
```python
import functools
import math

import jax
import jax.numpy as jnp
from jax import lax
from jax.experimental import pallas as pl
from jax.experimental.pallas import tpu as pltpu
from jax.sharding import Mesh, PartitionSpec as P

ITERS = 5
MOMENTUM_DECAY = 0.95
NORM_EPS = 1e-07
NEWTON_FIRST = 3.4445
NEWTON_SECOND = -4.775
NEWTON_THIRD = 2.0315
UPDATE_SCALE = 0.2
WEIGHT_DECAY = 0.1

LANES = 128
VMEM = pl.BlockSpec(memory_space=pltpu.VMEM)
PARAMS = pltpu.CompilerParams(vmem_limit_bytes=32 * 1024 * 1024)
NT = (((1,), (1,)), ((), ()))
NN = (((1,), (0,)), ((), ()))
TN = (((0,), (0,)), ((), ()))

def chip_index():
    y = lax.axis_index("y_high") * lax.axis_size("y_low") + lax.axis_index("y_low")
    return lax.axis_index("x") * (lax.axis_size("y_high") * lax.axis_size("y_low")) + y


def mm(a, b, dims, precision=None):
    return lax.dot_general(a, b, dims, precision=precision, preferred_element_type=jnp.float32)


def pair_sum_kernel(own_ref, other_ref, old_ref, out_ref):
    core, chip = lax.axis_index("core"), chip_index()
    for q in range(out_ref.shape[0]):
        lanes = slice(q * LANES, (q + 1) * LANES)
        total = own_ref[core, :, lanes].astype(jnp.float32) + other_ref[:, lanes].astype(jnp.float32)
        out_ref[q] = total.astype(jnp.bfloat16)
    cores, _, slab, height = old_ref.shape
    cols = cores * slab
    per_chunk = LANES // cols
    chunk, slot = chip // per_chunk, chip % per_chunk
    old = jnp.concatenate([old_ref[k, core] for k in range(cores)], axis=0)
    want = lax.broadcasted_iota(jnp.int32, (cols, LANES), 0) + slot * cols
    have = lax.broadcasted_iota(jnp.int32, (cols, LANES), 1)
    pick = (want == have).astype(jnp.float32)
    spread = mm(MOMENTUM_DECAY * old, pick, TN, lax.Precision.HIGHEST)
    lanes = pl.ds(pl.multiple_of(chunk * LANES, LANES), LANES)
    total = own_ref[core, :, lanes].astype(jnp.float32) + other_ref[:, lanes].astype(jnp.float32)
    out_ref[chunk] = (total + spread).astype(jnp.bfloat16)


def pair_sum(own, other, old):
    height, width = other.shape
    return pl.pallas_call(
        pair_sum_kernel,
        in_specs=[VMEM, VMEM, VMEM],
        out_specs=VMEM,
        out_shape=jax.ShapeDtypeStruct((width // LANES, height, LANES), jnp.bfloat16),
        compiler_params=PARAMS,
    )(own, other, old)


def add_parts(parts_ref):
    total = parts_ref[0].astype(jnp.float32)
    for k in range(1, parts_ref.shape[0]):
        total = total + parts_ref[k].astype(jnp.float32)
    return total


def sum_kernel(parts_ref, copies_ref):
    total = add_parts(parts_ref).astype(jnp.bfloat16)
    for k in range(copies_ref.shape[0]):
        copies_ref[k] = total


def sum_and_copy(parts, copies):
    return pl.pallas_call(
        sum_kernel,
        in_specs=[VMEM],
        out_specs=VMEM,
        out_shape=jax.ShapeDtypeStruct((copies,) + parts.shape[1:], jnp.bfloat16),
        compiler_params=PARAMS,
    )(parts)


def mask_kernel(mats, live_ref, parts_ref, copies_ref):
    total = add_parts(parts_ref)
    rows = lax.broadcasted_iota(jnp.int32, total.shape, 0)
    matrix = lax.axis_index("own") * mats + lax.axis_index("core")
    which = lax.broadcasted_iota(jnp.int32, live_ref.shape, 1) == matrix
    live = jnp.sum(jnp.where(which, live_ref[...], 0), axis=1, keepdims=True)
    new = jnp.where(rows < live, total, 0.0).astype(jnp.bfloat16)
    for k in range(copies_ref.shape[0]):
        copies_ref[k] = new


def sum_mask_and_copy(mats, live_rows, parts, copies):
    return pl.pallas_call(
        functools.partial(mask_kernel, mats),
        in_specs=[VMEM, VMEM],
        out_specs=VMEM,
        out_shape=jax.ShapeDtypeStruct((copies,) + parts.shape[1:], jnp.bfloat16),
        compiler_params=PARAMS,
    )(live_rows[None, :], parts)


def newton_kernel(gathered_ref, out_ref, x_ref):
    chunks, height, _ = gathered_ref.shape
    cols = out_ref.shape[1]
    per_chunk = LANES // cols
    chunk, slot = chip_index() // per_chunk, chip_index() % per_chunk
    want = lax.broadcasted_iota(jnp.int32, (cols, LANES), 0) + slot * cols
    have = lax.broadcasted_iota(jnp.int32, (cols, LANES), 1)
    pick = (want == have).astype(jnp.bfloat16)
    out_ref[0] = mm(pick, gathered_ref[chunk], NT)
    row = lax.broadcasted_iota(jnp.int32, (height, height), 0)
    col = lax.broadcasted_iota(jnp.int32, (height, height), 1)
    source = gathered_ref
    for step in range(ITERS):
        x = jnp.concatenate([source[q] for q in range(chunks)], axis=1)
        gram = mm(x, x, NT)
        if step == 0:
            norm = jnp.sqrt(jnp.sum(jnp.where(row == col, gram, 0.0), keepdims=True))
            scale = 1.0 / (norm + NORM_EPS)
            gram = gram * scale * scale
        gram = gram.astype(jnp.bfloat16)
        square = mm(gram, gram, NN)
        poly = (NEWTON_SECOND * gram.astype(jnp.float32) + NEWTON_THIRD * square).astype(jnp.bfloat16)
        if step == ITERS - 1:
            mine = mm(pick, x_ref[chunk], NT)
            out_ref[1] = NEWTON_FIRST * mine + mm(mine.astype(jnp.bfloat16), poly, NT)
            break
        for q in range(0, chunks, 2):
            part = jnp.concatenate([source[q], source[q + 1]], axis=1)
            part = NEWTON_FIRST * part.astype(jnp.float32) + mm(poly, part, NN)
            if step == 0:
                part = part * scale
            part = part.astype(jnp.bfloat16)
            x_ref[q] = part[:, :LANES]
            x_ref[q + 1] = part[:, LANES:]
        source = x_ref


def newton(gathered, cols):
    return pl.pallas_call(
        newton_kernel,
        in_specs=[VMEM],
        out_specs=VMEM,
        out_shape=jax.ShapeDtypeStruct((2, cols, gathered.shape[1]), jnp.float32),
        scratch_shapes=[pltpu.VMEM(gathered.shape, jnp.bfloat16)],
        compiler_params=PARAMS,
    )(gathered)


def finish_kernel(factor, back_ref, weights_ref, new_ref, update_ref):
    mats, slab, _ = weights_ref.shape
    mine = pl.ds(pl.multiple_of(lax.axis_index("core") * slab, slab), slab)
    for m in range(mats):
        new_ref[m] = back_ref[m, 0, mine, :]
        update_ref[m] = factor * back_ref[m, 1, mine, :] + WEIGHT_DECAY * weights_ref[m]


def finish(back, weights, factor):
    def kernel(*refs):
        finish_kernel(factor, *refs)

    shape = jax.ShapeDtypeStruct(weights.shape, jnp.float32)
    return pl.pallas_call(
        kernel,
        in_specs=[VMEM, VMEM],
        out_specs=[VMEM, VMEM],
        out_shape=[shape, shape],
        compiler_params=PARAMS,
    )(back, weights)


def per_device(grads, momentum, weights, live_rows):
    mats, height, slab = momentum.shape
    cores = lax.axis_size("core")
    width = grads.shape[3]
    core = lax.axis_index("core")
    group = ("x", "y_low")
    given = lax.dynamic_index_in_dim(grads[0], cores - 1 - core, 0, keepdims=False)
    other = lax.ppermute(given, "core", [(0, 1), (1, 0)])
    old = lax.all_gather(jnp.swapaxes(momentum, 1, 2), "core")
    chunks = pair_sum(grads[0], other, old)
    chunks = lax.all_to_all(chunks, group, 0, 0)
    chunk = sum_and_copy(chunks, lax.axis_size("y_high"))
    chunk = lax.all_to_all(chunk, "y_high", 0, 0)
    copies = sum_mask_and_copy(mats, live_rows, chunk, width // LANES)
    gathered = lax.all_to_all(copies, group, 0, 0)
    mine = newton(gathered, cores * slab)
    back = lax.all_gather(mine, "core")
    new_momentum, update = finish(
        back, jnp.swapaxes(weights, 1, 2), UPDATE_SCALE * math.sqrt(width)
    )
    return (jnp.swapaxes(new_momentum, 1, 2), jnp.swapaxes(update, 1, 2))


def solution(mesh):
    fsdp, own = mesh.devices.shape
    assert (fsdp, own) == (64, 12)
    split = Mesh(mesh.devices.reshape(4, 4, 2, 2, own), ("x", "y_high", "y_low", "core", "own"))
    all_fsdp = ("x", "y_high", "y_low", "core")
    in_specs = (P(all_fsdp, "own", None, None), P("own", None, all_fsdp), P("own", None, all_fsdp), P())
    out_specs = (P("own", None, all_fsdp), P("own", None, all_fsdp))
    return jax.shard_map(
        per_device, mesh=split, in_specs=in_specs, out_specs=out_specs, check_vma=False
    )
```

time: 68.1 us -> 65.5 us (0.962)
  Pallas kernels: 8.97 us -> 6.34 us
    pallas_call x4, Pallas kernels: 8.89 us -> 6.26 us  [the longest x1 4.95 us: newton(): pl.pallas_call(newton_kernel, in_specs=[VMEM], out_specs=VMEM, out_shape=...]
where the time goes in v3:
time: 65.5 us; the launch traced here: 65.2 us
  blocking collectives  44.5 us (68%)
  starting transfers between devices  12.4 us (19%)
  Pallas kernels  6.34 us (10%)
  local copies, waits for them, and re-layouts  1.22 us (2%)
  between operations  0.7 us (1%)
    all_to_all x1, blocking collectives, per_device(): chunks = lax.all_to_all(chunks, group, 0, 0)  13.2 us
    all_to_all x1, blocking collectives, per_device(): gathered = lax.all_to_all(copies, group, 0, 0)  12.6 us
    ppermute x1, starting transfers between devices, per_device(): other = lax.ppermute(given, 'core', [(0, 1), (1, 0)])  12.4 us
    all_to_all x1, blocking collectives, per_device(): chunk = lax.all_to_all(chunk, 'y_high', 0, 0)  11.6 us
    all_gather x1, blocking collectives, per_device(): back = lax.all_gather(mine, 'core')  5.06 us
    pallas_call x1, Pallas kernels, newton(): pl.pallas_call(newton_kernel, in_specs=[VMEM], out_specs=VMEM, out_shape=...  4.95 us
    all_gather x1, blocking collectives, per_device(): old = lax.all_gather(jnp.swapaxes(momentum, 1, 2), 'core')  2.09 us
  transfers between devices with their start and end apart: 1, of which 0 were waited for; matrix products, arithmetic and copies ran while one was open for 0% of the time, Pallas kernels for 0%

profile of v3, /device:TPU:1, one launch (start us, length us, event | category | flops | bytes accessed | tf_op | source)
XLA Modules:
  0.0 65.2 jit_solution(8819415196259325333)
XLA Ops:
  0.6 0.0 copy-start
  0.6 1.2 %dynamic-slice_bitcast_fusion = bf16[288,1024]{1,0:T(8,128)(2,1)S(1)} fusion(bf16[1,2,288,1024]{3,2,1,0:T(8,128)(2,1)} %param.4, s32[]{:T(128)S(6)} %select_n.4), kind=kLoop, calls=%fused_computation | loop fusion | bytes 1179652 | tf_op jit(solution)/shard_map/jit(dynamic_index_in_dim)/squeeze | solution.py:187
  1.8 12.4 %collective-permute-start = (bf16[288,1024]{1,0:T(8,128)(2,1)S(1)}, bf16[288,1024]{1,0:T(8,128)(2,1)S(1)}, u32[]{:S(2)}, u32[]{:S(2)}) collective-permute-start(bf16[288,1024]{1,0:T(8,128)(2,1)S(1)} %dynamic-slice_bitcast_fusion), channel_id=1, source_target_pairs={{0,12},{12,0},{1,13},{13,1},{2,14},{14,2},{3,15},{15,3},{4,16},{16... | collective-permute-start | bytes 1769480 | tf_op jit(solution)/shard_map/ppermute | solution.py:188
  14.3 2.1 %all-gather = f32[4,16,288]{2,1,0:T(8,128)S(1)} all-gather(f32[2,16,288]{2,1,0:T(8,128)} %bitcast.15), channel_id=2, replica_groups=mesh['x'=4,'y_high'=4,'y_low'=2,'core'=2,'own'=12] {'core'}, dimensions={0}, use_global_device_ids=true | all-gather | bytes 110592 | tf_op jit(solution)/shard_map/all_gather | solution.py:189
  16.4 0.0 collective-permute-done.other_ref
  16.4 0.0 copy-done
  16.4 0.5 shard_map.59
  16.9 0.0 copy-start.2
  16.9 13.2 %all_to_all.15.parts_ref = bf16[8,288,128]{2,1,0:T(8,128)(2,1)S(1)} all-to-all(bf16[8,288,128]{2,1,0:T(8,128)(2,1)S(1)} %shard_map.59), channel_id=1, replica_groups=mesh['x'=4,'y_high'=4,'y_low'=2,'core'=2,'own'=12] {'x','y_low'}, dimensions={0} | all-to-all | bytes 1179648 | tf_op jit(solution)/shard_map/all_to_all | solution.py:191
  30.1 0.1 shard_map.60
  30.1 11.6 %all_to_all.16.parts_ref = bf16[4,288,128]{2,1,0:T(8,128)(2,1)S(1)} all-to-all(bf16[4,288,128]{2,1,0:T(8,128)(2,1)S(1)} %shard_map.60), channel_id=1, replica_groups=mesh['x'=4,'y_high'=4,'y_low'=2,'core'=2,'own'=12] {'y_high'}, dimensions={0} | all-to-all | bytes 589824 | tf_op jit(solution)/shard_map/all_to_all | solution.py:193
  41.8 0.0 copy-done.2
  41.8 0.1 shard_map.61
  41.9 0.0 copy-start.1
  41.9 12.6 %all_to_all.17.gathered_ref = bf16[8,288,128]{2,1,0:T(8,128)(2,1)S(1)} all-to-all(bf16[8,288,128]{2,1,0:T(8,128)(2,1)S(1)} %shard_map.61), channel_id=1, replica_groups=mesh['x'=4,'y_high'=4,'y_low'=2,'core'=2,'own'=12] {'x','y_low'}, dimensions={0} | all-to-all | bytes 1179648 | tf_op jit(solution)/shard_map/all_to_all | solution.py:195
  54.5 4.9 %shard_map.62 = f32[2,32,288]{2,1,0:T(8,128)S(1)} custom-call(bf16[8,288,128]{2,1,0:T(8,128)(2,1)S(1)} %all_to_all.17.gathered_ref), custom_call_target="tpu_custom_call" | custom-call | tf_op jit(solution)/shard_map/pallas_call | solution.py:149
  59.5 5.1 %all-gather.1 = f32[4,32,288]{2,1,0:T(8,128)S(1)} all-gather(f32[2,32,288]{2,1,0:T(8,128)S(1)} %shard_map.62), channel_id=3, replica_groups=mesh['x'=4,'y_high'=4,'y_low'=2,'core'=2,'own'=12] {'core'}, dimensions={0}, use_global_device_ids=true | all-gather | bytes 221184 | tf_op jit(solution)/shard_map/all_gather | solution.py:197
  64.5 0.0 copy-done.1
  64.5 0.6 shard_map.63
Async XLA Ops:
  0.6 15.7 %copy-start = (bf16[1,2,288,1024]{3,2,1,0:T(8,128)(2,1)S(1)}, bf16[1,2,288,1024]{3,2,1,0:T(8,128)(2,1)}, u32[]{:S(2)}) copy-start(bf16[1,2,288,1024]{3,2,1,0:T(8,128)(2,1)} %param.4) | copy-start | bytes 3538948
  1.8 14.5 %collective-permute-start = (bf16[288,1024]{1,0:T(8,128)(2,1)S(1)}, bf16[288,1024]{1,0:T(8,128)(2,1)S(1)}, u32[]{:S(2)}, u32[]{:S(2)}) collective-permute-start(bf16[288,1024]{1,0:T(8,128)(2,1)S(1)} %dynamic-slice_bitcast_fusion), channel_id=1, source_target_pairs={{0,12},{12,0},{1,13},{13,1},{2,14},{14,2},{3,15},{15,3},{4,16},{16... | collective-permute-start | bytes 1769480 | tf_op jit(solution)/shard_map/ppermute | solution.py:188
  16.9 24.9 %copy-start.2 = (s32[24]{0:T(128)S(1)}, s32[24]{0:T(128)}, u32[]{:S(2)}) copy-start(s32[24]{0:T(128)} %param.7) | copy-start | bytes 292
  41.9 22.6 %copy-start.1 = (f32[2,288,16]{1,2,0:T(8,128)S(1)}, f32[2,288,16]{1,2,0:T(8,128)}, u32[]{:S(2)}) copy-start(f32[2,288,16]{1,2,0:T(8,128)} %param.6) | copy-start | bytes 110596

commit v4 on v3

--- a/solution.py
+++ b/solution.py
@@ -35,9 +35,10 @@
 
 def pair_sum_kernel(own_ref, other_ref, old_ref, out_ref):
     core, chip = lax.axis_index("core"), chip_index()
+    rows = out_ref.shape[1]
     for q in range(out_ref.shape[0]):
         lanes = slice(q * LANES, (q + 1) * LANES)
-        total = own_ref[core, :, lanes].astype(jnp.float32) + other_ref[:, lanes].astype(jnp.float32)
+        total = own_ref[core, :rows, lanes].astype(jnp.float32) + other_ref[:rows, lanes].astype(jnp.float32)
         out_ref[q] = total.astype(jnp.bfloat16)
     cores, _, slab, height = old_ref.shape
     cols = cores * slab
@@ -47,19 +48,19 @@
     want = lax.broadcasted_iota(jnp.int32, (cols, LANES), 0) + slot * cols
     have = lax.broadcasted_iota(jnp.int32, (cols, LANES), 1)
     pick = (want == have).astype(jnp.float32)
-    spread = mm(MOMENTUM_DECAY * old, pick, TN, lax.Precision.HIGHEST)
+    spread = mm(MOMENTUM_DECAY * old, pick, TN, lax.Precision.HIGHEST)[:rows]
     lanes = pl.ds(pl.multiple_of(chunk * LANES, LANES), LANES)
-    total = own_ref[core, :, lanes].astype(jnp.float32) + other_ref[:, lanes].astype(jnp.float32)
+    total = own_ref[core, :rows, lanes].astype(jnp.float32) + other_ref[:rows, lanes].astype(jnp.float32)
     out_ref[chunk] = (total + spread).astype(jnp.bfloat16)
 
 
-def pair_sum(own, other, old):
-    height, width = other.shape
+def pair_sum(own, other, old, rows):
+    width = other.shape[1]
     return pl.pallas_call(
         pair_sum_kernel,
         in_specs=[VMEM, VMEM, VMEM],
         out_specs=VMEM,
-        out_shape=jax.ShapeDtypeStruct((width // LANES, height, LANES), jnp.bfloat16),
+        out_shape=jax.ShapeDtypeStruct((width // LANES, rows, LANES), jnp.bfloat16),
         compiler_params=PARAMS,
     )(own, other, old)
 
@@ -116,7 +117,12 @@
     want = lax.broadcasted_iota(jnp.int32, (cols, LANES), 0) + slot * cols
     have = lax.broadcasted_iota(jnp.int32, (cols, LANES), 1)
     pick = (want == have).astype(jnp.bfloat16)
-    out_ref[0] = mm(pick, gathered_ref[chunk], NT)
+    past = jnp.zeros((cols, out_ref.shape[2] - height), jnp.float32)
+
+    def write(k, value):
+        out_ref[k] = jnp.concatenate([value, past], axis=1) if past.shape[1] else value
+
+    write(0, mm(pick, gathered_ref[chunk], NT))
     row = lax.broadcasted_iota(jnp.int32, (height, height), 0)
     col = lax.broadcasted_iota(jnp.int32, (height, height), 1)
     source = gathered_ref
@@ -132,7 +138,7 @@
         poly = (NEWTON_SECOND * gram.astype(jnp.float32) + NEWTON_THIRD * square).astype(jnp.bfloat16)
         if step == ITERS - 1:
             mine = mm(pick, x_ref[chunk], NT)
-            out_ref[1] = NEWTON_FIRST * mine + mm(mine.astype(jnp.bfloat16), poly, NT)
+            write(1, NEWTON_FIRST * mine + mm(mine.astype(jnp.bfloat16), poly, NT))
             break
         for q in range(0, chunks, 2):
             part = jnp.concatenate([source[q], source[q + 1]], axis=1)
@@ -145,12 +151,12 @@
         source = x_ref
 
 
-def newton(gathered, cols):
+def newton(gathered, cols, height):
     return pl.pallas_call(
         newton_kernel,
         in_specs=[VMEM],
         out_specs=VMEM,
-        out_shape=jax.ShapeDtypeStruct((2, cols, gathered.shape[1]), jnp.float32),
+        out_shape=jax.ShapeDtypeStruct((2, cols, height), jnp.float32),
         scratch_shapes=[pltpu.VMEM(gathered.shape, jnp.bfloat16)],
         compiler_params=PARAMS,
     )(gathered)
@@ -187,13 +193,19 @@
     given = lax.dynamic_index_in_dim(grads[0], cores - 1 - core, 0, keepdims=False)
     other = lax.ppermute(given, "core", [(0, 1), (1, 0)])
     old = lax.all_gather(jnp.swapaxes(momentum, 1, 2), "core")
-    chunks = pair_sum(grads[0], other, old)
-    chunks = lax.all_to_all(chunks, group, 0, 0)
-    chunk = sum_and_copy(chunks, lax.axis_size("y_high"))
-    chunk = lax.all_to_all(chunk, "y_high", 0, 0)
-    copies = sum_mask_and_copy(mats, live_rows, chunk, width // LANES)
-    gathered = lax.all_to_all(copies, group, 0, 0)
-    mine = newton(gathered, cores * slab)
+    def chain(rows):
+        chunks = pair_sum(grads[0], other, old, rows)
+        chunks = lax.all_to_all(chunks, group, 0, 0)
+        chunk = sum_and_copy(chunks, lax.axis_size("y_high"))
+        chunk = lax.all_to_all(chunk, "y_high", 0, 0)
+        copies = sum_mask_and_copy(mats, live_rows, chunk, width // LANES)
+        gathered = lax.all_to_all(copies, group, 0, 0)
+        return newton(gathered, cores * slab, height)
+
+    live = lax.dynamic_index_in_dim(live_rows, lax.axis_index("own") * mats + core, 0, keepdims=False)
+    counts = [192, 240, height]
+    level = sum((live > rows).astype(jnp.int32) for rows in counts[:-1])
+    mine = lax.switch(level, [functools.partial(chain, rows) for rows in counts])
     back = lax.all_gather(mine, "core")
     new_momentum, update = finish(
         back, jnp.swapaxes(weights, 1, 2), UPDATE_SCALE * math.sqrt(width)

time: 65.5 us -> 62.9 us (0.960)
  blocking collectives: 44.5 us -> 40.8 us
  between operations: 0.7 us -> 2 us
  Pallas kernels: 6.34 us -> 5.26 us
    all_to_all x3, blocking collectives: 37.3 us -> 33.4 us  [the longest x1 12.1 us: chain(): chunks = lax.all_to_all(chunks, group, 0, 0)]
    pallas_call x1, Pallas kernels: 4.95 us -> 3.94 us  [newton(): pl.pallas_call(newton_kernel, in_specs=[VMEM], out_specs=VMEM, out_shape=...]
  transfers between devices with their start and end apart: 1 -> 1, of which waited for: 0 -> 0; matrix products, arithmetic and copies ran while one was open for 0% -> 1% of each run, Pallas kernels for 0% -> 0%
where the time goes in v4:
time: 62.9 us; the launch traced here: 62.3 us
  blocking collectives  40.8 us (65%)
  starting transfers between devices  12.4 us (20%)
  Pallas kernels  5.26 us (8%)
  between operations  2 us (3%)
  local copies, waits for them, and re-layouts  1.8 us (3%)
    ppermute x1, starting transfers between devices, per_device(): other = lax.ppermute(given, 'core', [(0, 1), (1, 0)])  12.4 us
    all_to_all x1, blocking collectives, chain(): chunks = lax.all_to_all(chunks, group, 0, 0)  12.1 us
    all_to_all x1, blocking collectives, chain(): chunk = lax.all_to_all(chunk, 'y_high', 0, 0)  10.9 us
    all_to_all x1, blocking collectives, chain(): gathered = lax.all_to_all(copies, group, 0, 0)  10.4 us
    all_gather x1, blocking collectives, per_device(): back = lax.all_gather(mine, 'core')  5.31 us
    pallas_call x1, Pallas kernels, newton(): pl.pallas_call(newton_kernel, in_specs=[VMEM], out_specs=VMEM, out_shape=...  3.94 us
    all_gather x1, blocking collectives, per_device(): old = lax.all_gather(jnp.swapaxes(momentum, 1, 2), 'core')  2.09 us
  transfers between devices with their start and end apart: 1, of which 0 were waited for; matrix products, arithmetic and copies ran while one was open for 1% of the time, Pallas kernels for 0%

profile of v4, /device:TPU:1, one launch (start us, length us, event | category | flops | bytes accessed | tf_op | source)
XLA Modules:
  0.0 62.3 jit_solution(6519063533513463109)
XLA Ops:
  0.6 0.0 copy-start.1
  0.6 0.0 copy-start.2
  0.7 1.2 %dynamic-slice_bitcast_fusion = bf16[288,1024]{1,0:T(8,128)(2,1)S(1)} fusion(bf16[1,2,288,1024]{3,2,1,0:T(8,128)(2,1)} %param.7, s32[]{:T(128)S(6)} %select_n.9), kind=kLoop, calls=%fused_computation | loop fusion | bytes 1179652 | tf_op jit(solution)/shard_map/jit(dynamic_index_in_dim)/squeeze | solution.py:193
  1.9 12.4 %collective-permute-start = (bf16[288,1024]{1,0:T(8,128)(2,1)S(1)}, bf16[288,1024]{1,0:T(8,128)(2,1)S(1)}, u32[]{:S(2)}, u32[]{:S(2)}) collective-permute-start(bf16[288,1024]{1,0:T(8,128)(2,1)S(1)} %dynamic-slice_bitcast_fusion), channel_id=1, source_target_pairs={{0,12},{12,0},{1,13},{13,1},{2,14},{14,2},{3,15},{15,3},{4,16},{16... | collective-permute-start | bytes 1769480 | tf_op jit(solution)/shard_map/ppermute | solution.py:194
  14.3 0.0 copy-done.2
  14.3 0.6 dynamic_slice.8
  16.2 2.1 %all-gather = f32[4,16,288]{2,1,0:T(8,128)S(1)} all-gather(f32[2,16,288]{2,1,0:T(8,128)} %bitcast.23), channel_id=2, replica_groups=mesh['x'=4,'y_high'=4,'y_low'=2,'core'=2,'own'=12] {'core'}, dimensions={0}, use_global_device_ids=true | all-gather | bytes 110592 | tf_op jit(solution)/shard_map/all_gather | solution.py:195
  18.3 0.0 collective-permute-done
  18.3 0.0 copy-done.1
  18.3 0.0 copy-start
  18.3 38.0 %conditional.1 = (f32[2,32,288]{2,1,0:T(8,128)S(1)}) conditional(s32[]{:T(128)} %bitcast.6, (s32[24]{0:T(128)S(1)}, bf16[1,2,288,1024]{3,2,1,0:T(8,128)(2,1)S(1)}, bf16[288,1024]{1,0:T(8,128)(2,1)S(1)}, f32[2,2,16,288]{3,2,1,0:T(8,128)S(1)}) %tuple.28, (s32[24]{0:T(128)S(1)}, bf16[1,2,288,1024]{3,2,1,0:T(8,128)(2,1)S(1)}, ...), branch_computations={%region_0.1_spmd, %region_1.2_spmd, %region_2.3_spmd} | conditional | bytes 2949128 | solution.py:208
  18.3 0.5 branch_1_fun.4
  18.8 12.1 %all_to_all.39.parts_ref = bf16[8,240,128]{2,1,0:T(8,128)(2,1)S(1)} all-to-all(bf16[8,240,128]{2,1,0:T(8,128)(2,1)S(1)} %branch_1_fun.4), channel_id=1, replica_groups=mesh['x'=4,'y_high'=4,'y_low'=2,'core'=2,'own'=12] {'x','y_low'}, dimensions={0} | all-to-all | bytes 983040 | tf_op jit(solution)/shard_map/cond/branch_1_fun/all_to_all | solution.py:198
  30.9 0.1 branch_1_fun.5
  31.0 10.9 %all_to_all.40.parts_ref = bf16[4,240,128]{2,1,0:T(8,128)(2,1)S(1)} all-to-all(bf16[4,240,128]{2,1,0:T(8,128)(2,1)S(1)} %branch_1_fun.5), channel_id=1, replica_groups=mesh['x'=4,'y_high'=4,'y_low'=2,'core'=2,'own'=12] {'y_high'}, dimensions={0} | all-to-all | bytes 491520 | tf_op jit(solution)/shard_map/cond/branch_1_fun/all_to_all | solution.py:200
  41.9 0.1 branch_1_fun.6
  42.0 10.4 %all_to_all.41.gathered_ref = bf16[8,240,128]{2,1,0:T(8,128)(2,1)S(1)} all-to-all(bf16[8,240,128]{2,1,0:T(8,128)(2,1)S(1)} %branch_1_fun.6), channel_id=1, replica_groups=mesh['x'=4,'y_high'=4,'y_low'=2,'core'=2,'own'=12] {'x','y_low'}, dimensions={0} | all-to-all | bytes 983040 | tf_op jit(solution)/shard_map/cond/branch_1_fun/all_to_all | solution.py:202
  52.4 3.9 %branch_1_fun.7 = f32[2,32,288]{2,1,0:T(8,128)S(1)} custom-call(bf16[8,240,128]{2,1,0:T(8,128)(2,1)S(1)} %all_to_all.41.gathered_ref), custom_call_target="tpu_custom_call" | custom-call | tf_op jit(solution)/shard_map/cond/branch_1_fun/pallas_call | solution.py:155
  56.4 5.3 %all-gather.1 = f32[4,32,288]{2,1,0:T(8,128)S(1)} all-gather(f32[2,32,288]{2,1,0:T(8,128)S(1)} %get-tuple-element.46), channel_id=3, replica_groups=mesh['x'=4,'y_high'=4,'y_low'=2,'core'=2,'own'=12] {'core'}, dimensions={0}, use_global_device_ids=true | all-gather | bytes 221184 | tf_op jit(solution)/shard_map/all_gather | solution.py:209
  61.7 0.0 copy-done
  61.7 0.6 %shard_map.59 = (f32[2,16,288]{2,1,0:T(8,128)}, f32[2,16,288]{2,1,0:T(8,128)}) custom-call(f32[2,2,32,288]{3,2,1,0:T(8,128)S(1)} %bitcast.15, f32[2,16,288]{2,1,0:T(8,128)S(1)} %bitcast.16), custom_call_target="tpu_custom_call" | custom-call | tf_op jit(solution)/shard_map/pallas_call | solution.py:178
Async XLA Ops:
  0.6 17.7 %copy-start.1 = (bf16[1,2,288,1024]{3,2,1,0:T(8,128)(2,1)S(1)}, bf16[1,2,288,1024]{3,2,1,0:T(8,128)(2,1)}, u32[]{:S(2)}) copy-start(bf16[1,2,288,1024]{3,2,1,0:T(8,128)(2,1)} %param.7) | copy-start | bytes 3538948
  0.6 13.7 %copy-start.2 = (s32[24]{0:T(128)S(1)}, s32[24]{0:T(128)}, u32[]{:S(2)}) copy-start(s32[24]{0:T(128)} %param.10) | copy-start | bytes 292
  1.9 16.4 %collective-permute-start = (bf16[288,1024]{1,0:T(8,128)(2,1)S(1)}, bf16[288,1024]{1,0:T(8,128)(2,1)S(1)}, u32[]{:S(2)}, u32[]{:S(2)}) collective-permute-start(bf16[288,1024]{1,0:T(8,128)(2,1)S(1)} %dynamic-slice_bitcast_fusion), channel_id=1, source_target_pairs={{0,12},{12,0},{1,13},{13,1},{2,14},{14,2},{3,15},{15,3},{4,16},{16... | collective-permute-start | bytes 1769480 | tf_op jit(solution)/shard_map/ppermute | solution.py:194
  18.3 43.4 %copy-start = (f32[2,288,16]{1,2,0:T(8,128)S(1)}, f32[2,288,16]{1,2,0:T(8,128)}, u32[]{:S(2)}) copy-start(f32[2,288,16]{1,2,0:T(8,128)} %param.9) | copy-start | bytes 110596

commit v5 on v4

--- a/solution.py
+++ b/solution.py
@@ -33,25 +33,46 @@
     return lax.dot_general(a, b, dims, precision=precision, preferred_element_type=jnp.float32)
 
 
+def spread_old(old):
+    slab, _ = old.shape
+    column = chip_index() * lax.axis_size("core") + lax.axis_index("core")
+    per_chunk = LANES // slab
+    want = lax.broadcasted_iota(jnp.int32, (slab, LANES), 0) + column % per_chunk * slab
+    have = lax.broadcasted_iota(jnp.int32, (slab, LANES), 1)
+    pick = (want == have).astype(jnp.float32)
+    chunk = column // per_chunk
+    lanes = pl.ds(pl.multiple_of(chunk * LANES, LANES), LANES)
+    return mm(MOMENTUM_DECAY * old, pick, TN, lax.Precision.HIGHEST), chunk, lanes
+
+
+def take_kernel(grads_ref, old_ref, out_ref):
+    other = 1 - lax.axis_index("core")
+    out_ref[...] = grads_ref[other]
+    spread, _, lanes = spread_old(old_ref[other])
+    out_ref[:, lanes] = (grads_ref[other, :, lanes].astype(jnp.float32) + spread).astype(jnp.bfloat16)
+
+
+def take_other(grads, old):
+    return pl.pallas_call(
+        take_kernel,
+        in_specs=[VMEM, VMEM],
+        out_specs=VMEM,
+        out_shape=jax.ShapeDtypeStruct(grads.shape[1:], grads.dtype),
+        compiler_params=PARAMS,
+    )(grads, old)
+
+
 def pair_sum_kernel(own_ref, other_ref, old_ref, out_ref):
-    core, chip = lax.axis_index("core"), chip_index()
+    core = lax.axis_index("core")
     rows = out_ref.shape[1]
+
+    def total(lanes):
+        return own_ref[core, :rows, lanes].astype(jnp.float32) + other_ref[:rows, lanes].astype(jnp.float32)
+
     for q in range(out_ref.shape[0]):
-        lanes = slice(q * LANES, (q + 1) * LANES)
-        total = own_ref[core, :rows, lanes].astype(jnp.float32) + other_ref[:rows, lanes].astype(jnp.float32)
-        out_ref[q] = total.astype(jnp.bfloat16)
-    cores, _, slab, height = old_ref.shape
-    cols = cores * slab
-    per_chunk = LANES // cols
-    chunk, slot = chip // per_chunk, chip % per_chunk
-    old = jnp.concatenate([old_ref[k, core] for k in range(cores)], axis=0)
-    want = lax.broadcasted_iota(jnp.int32, (cols, LANES), 0) + slot * cols
-    have = lax.broadcasted_iota(jnp.int32, (cols, LANES), 1)
-    pick = (want == have).astype(jnp.float32)
-    spread = mm(MOMENTUM_DECAY * old, pick, TN, lax.Precision.HIGHEST)[:rows]
-    lanes = pl.ds(pl.multiple_of(chunk * LANES, LANES), LANES)
-    total = own_ref[core, :rows, lanes].astype(jnp.float32) + other_ref[:rows, lanes].astype(jnp.float32)
-    out_ref[chunk] = (total + spread).astype(jnp.bfloat16)
+        out_ref[q] = total(slice(q * LANES, (q + 1) * LANES)).astype(jnp.bfloat16)
+    spread, chunk, lanes = spread_old(old_ref[core])
+    out_ref[chunk] = (total(lanes) + spread[:rows]).astype(jnp.bfloat16)
 
 
 def pair_sum(own, other, old, rows):
@@ -190,9 +211,8 @@
     width = grads.shape[3]
     core = lax.axis_index("core")
     group = ("x", "y_low")
-    given = lax.dynamic_index_in_dim(grads[0], cores - 1 - core, 0, keepdims=False)
-    other = lax.ppermute(given, "core", [(0, 1), (1, 0)])
-    old = lax.all_gather(jnp.swapaxes(momentum, 1, 2), "core")
+    old = jnp.swapaxes(momentum, 1, 2)
+    other = lax.ppermute(take_other(grads[0], old), "core", [(0, 1), (1, 0)])
     def chain(rows):
         chunks = pair_sum(grads[0], other, old, rows)
         chunks = lax.all_to_all(chunks, group, 0, 0)

time: 62.9 us -> 62.7 us (level)
  Pallas kernels: 5.26 us -> 6.5 us
  local copies, waits for them, and re-layouts: 1.8 us -> 0.61 us
    all_gather x1, blocking collectives: 5.31 us -> 9.96 us  [per_device(): back = lax.all_gather(mine, 'core')]
    all_gather x1 -> x0, blocking collectives: 2.09 us -> none  [per_device(): old = lax.all_gather(jnp.swapaxes(momentum, 1, 2), 'core')]
    pallas_call x0 -> x1, Pallas kernels: none -> 1.69 us  [take_other(): pl.pallas_call(take_kernel, in_specs=[VMEM, VMEM], out_specs=VMEM, out_sh...]
    squeeze x1 -> x0, local copies, waits for them, and re-layouts: 1.2 us -> none  [per_device(): lax.dynamic_index_in_dim(grads[0], cores - 1 - core, 0, keepdims=False)]
    all_to_all x1, blocking collectives: 12.1 us -> 11 us  [chain(): chunks = lax.all_to_all(chunks, group, 0, 0)]
    all_to_all x1, blocking collectives: 10.4 us -> 9.61 us  [chain(): gathered = lax.all_to_all(copies, group, 0, 0)]
where the time goes in v5:
time: 62.7 us; the launch traced here: 62.4 us
  blocking collectives  40.8 us (65%)
  starting transfers between devices  12.4 us (20%)
  Pallas kernels  6.5 us (10%)
  between operations  2.03 us (3%)
    ppermute x1, starting transfers between devices, per_device(): other = lax.ppermute(take_other(grads[0], old), 'core', [(0, 1), (1, 0)])  12.4 us
    all_to_all x1, blocking collectives, chain(): chunks = lax.all_to_all(chunks, group, 0, 0)  11 us
    all_to_all x1, blocking collectives, chain(): chunk = lax.all_to_all(chunk, 'y_high', 0, 0)  10.3 us
    all_gather x1, blocking collectives, per_device(): back = lax.all_gather(mine, 'core')  9.96 us
    all_to_all x1, blocking collectives, chain(): gathered = lax.all_to_all(copies, group, 0, 0)  9.61 us
    pallas_call x1, Pallas kernels, newton(): pl.pallas_call(newton_kernel, in_specs=[VMEM], out_specs=VMEM, out_shape=...  3.56 us
    pallas_call x1, Pallas kernels, take_other(): pl.pallas_call(take_kernel, in_specs=[VMEM, VMEM], out_specs=VMEM, out_sh...  1.69 us
  transfers between devices with their start and end apart: 1, of which 0 were waited for; matrix products, arithmetic and copies ran while one was open for 1% of the time, Pallas kernels for 0%

profile of v5, /device:TPU:1, one launch (start us, length us, event | category | flops | bytes accessed | tf_op | source)
XLA Modules:
  0.0 62.4 jit_solution(1747689978358084683)
XLA Ops:
  0.6 0.0 copy-start.1
  0.6 0.0 copy-start.2
  0.6 0.0 copy-start.3
  0.7 1.7 %shard_map.59 = bf16[288,1024]{1,0:T(8,128)(2,1)S(1)} custom-call(bf16[2,288,1024]{2,1,0:T(8,128)(2,1)} %bitcast.15, f32[2,16,288]{2,1,0:T(8,128)} %bitcast.19), custom_call_target="tpu_custom_call" | custom-call | tf_op jit(solution)/shard_map/pallas_call | solution.py:56
  2.4 12.4 %collective-permute-start = (bf16[288,1024]{1,0:T(8,128)(2,1)S(1)}, bf16[288,1024]{1,0:T(8,128)(2,1)S(1)}, u32[]{:S(2)}, u32[]{:S(2)}) collective-permute-start(bf16[288,1024]{1,0:T(8,128)(2,1)S(1)} %shard_map.59), channel_id=1, source_target_pairs={{0,12},{12,0},{1,13},{13,1},{2,14},{14,2},{3,15},{15,3},{4,16},{16... | collective-permute-start | bytes 1769480 | tf_op jit(solution)/shard_map/ppermute | solution.py:215
  14.8 0.0 copy-done.3
  14.8 0.6 dynamic_slice.4
  16.7 0.0 collective-permute-done
  16.7 0.0 copy-done.1
  16.7 0.0 copy-done.2
  16.7 0.0 copy-start
  16.8 35.1 %conditional.1 = (f32[2,32,288]{2,1,0:T(8,128)S(1)}) conditional(s32[]{:T(128)} %bitcast.6, (s32[24]{0:T(128)S(1)}, bf16[1,2,288,1024]{3,2,1,0:T(8,128)(2,1)S(1)}, bf16[288,1024]{1,0:T(8,128)(2,1)S(1)}, f32[2,16,288]{2,1,0:T(8,128)S(1)}) %tuple.28, (s32[24]{0:T(128)S(1)}, bf16[1,2,288,1024]{3,2,1,0:T(8,128)(2,1)S(1)}, ...), branch_computations={%region_0.1_spmd, %region_1.2_spmd, %region_2.3_spmd} | conditional | bytes 2949128 | solution.py:228
  16.8 0.4 branch_0_fun.4
  17.2 11.0 %all_to_all.36.parts_ref = bf16[8,192,128]{2,1,0:T(8,128)(2,1)S(1)} all-to-all(bf16[8,192,128]{2,1,0:T(8,128)(2,1)S(1)} %branch_0_fun.4), channel_id=1, replica_groups=mesh['x'=4,'y_high'=4,'y_low'=2,'core'=2,'own'=12] {'x','y_low'}, dimensions={0} | all-to-all | bytes 786432 | tf_op jit(solution)/shard_map/cond/branch_0_fun/all_to_all | solution.py:218
  28.1 0.1 branch_0_fun.5
  28.2 10.3 %all_to_all.37.parts_ref = bf16[4,192,128]{2,1,0:T(8,128)(2,1)S(1)} all-to-all(bf16[4,192,128]{2,1,0:T(8,128)(2,1)S(1)} %branch_0_fun.5), channel_id=1, replica_groups=mesh['x'=4,'y_high'=4,'y_low'=2,'core'=2,'own'=12] {'y_high'}, dimensions={0} | all-to-all | bytes 393216 | tf_op jit(solution)/shard_map/cond/branch_0_fun/all_to_all | solution.py:220
  38.5 0.1 branch_0_fun.6
  38.6 9.6 %all_to_all.38.gathered_ref = bf16[8,192,128]{2,1,0:T(8,128)(2,1)S(1)} all-to-all(bf16[8,192,128]{2,1,0:T(8,128)(2,1)S(1)} %branch_0_fun.6), channel_id=1, replica_groups=mesh['x'=4,'y_high'=4,'y_low'=2,'core'=2,'own'=12] {'x','y_low'}, dimensions={0} | all-to-all | bytes 786432 | tf_op jit(solution)/shard_map/cond/branch_0_fun/all_to_all | solution.py:222
  48.2 3.6 %branch_0_fun.7 = f32[2,32,288]{2,1,0:T(8,128)S(1)} custom-call(bf16[8,192,128]{2,1,0:T(8,128)(2,1)S(1)} %all_to_all.38.gathered_ref), custom_call_target="tpu_custom_call" | custom-call | tf_op jit(solution)/shard_map/cond/branch_0_fun/pallas_call | solution.py:176
  51.8 10.0 %all-gather = f32[4,32,288]{2,1,0:T(8,128)S(1)} all-gather(f32[2,32,288]{2,1,0:T(8,128)S(1)} %get-tuple-element.46), channel_id=2, replica_groups=mesh['x'=4,'y_high'=4,'y_low'=2,'core'=2,'own'=12] {'core'}, dimensions={0}, use_global_device_ids=true | all-gather | bytes 221184 | tf_op jit(solution)/shard_map/all_gather | solution.py:229
  61.8 0.0 copy-done
  61.8 0.6 %shard_map.60 = (f32[2,16,288]{2,1,0:T(8,128)}, f32[2,16,288]{2,1,0:T(8,128)}) custom-call(f32[2,2,32,288]{3,2,1,0:T(8,128)S(1)} %bitcast.13, f32[2,16,288]{2,1,0:T(8,128)S(1)} %bitcast.14), custom_call_target="tpu_custom_call" | custom-call | tf_op jit(solution)/shard_map/pallas_call | solution.py:199
Async XLA Ops:
  0.6 16.1 %copy-start.1 = (bf16[1,2,288,1024]{3,2,1,0:T(8,128)(2,1)S(1)}, bf16[1,2,288,1024]{3,2,1,0:T(8,128)(2,1)}, u32[]{:S(2)}) copy-start(bf16[1,2,288,1024]{3,2,1,0:T(8,128)(2,1)} %param.7) | copy-start | bytes 3538948
  0.6 16.1 %copy-start.2 = (f32[2,288,16]{1,2,0:T(8,128)S(1)}, f32[2,288,16]{1,2,0:T(8,128)}, u32[]{:S(2)}) copy-start(f32[2,288,16]{1,2,0:T(8,128)} %param.8) | copy-start | bytes 110596
  0.6 14.2 %copy-start.3 = (s32[24]{0:T(128)S(1)}, s32[24]{0:T(128)}, u32[]{:S(2)}) copy-start(s32[24]{0:T(128)} %param.10) | copy-start | bytes 292
  2.4 14.4 %collective-permute-start = (bf16[288,1024]{1,0:T(8,128)(2,1)S(1)}, bf16[288,1024]{1,0:T(8,128)(2,1)S(1)}, u32[]{:S(2)}, u32[]{:S(2)}) collective-permute-start(bf16[288,1024]{1,0:T(8,128)(2,1)S(1)} %shard_map.59), channel_id=1, source_target_pairs={{0,12},{12,0},{1,13},{13,1},{2,14},{14,2},{3,15},{15,3},{4,16},{16... | collective-permute-start | bytes 1769480 | tf_op jit(solution)/shard_map/ppermute | solution.py:215
  16.7 45.0 %copy-start = (f32[2,288,16]{1,2,0:T(8,128)S(1)}, f32[2,288,16]{1,2,0:T(8,128)}, u32[]{:S(2)}) copy-start(f32[2,288,16]{1,2,0:T(8,128)} %param.9) | copy-start | bytes 110596

commit v6 on v5

--- a/solution.py
+++ b/solution.py
@@ -223,8 +223,9 @@
         return newton(gathered, cores * slab, height)
 
     live = lax.dynamic_index_in_dim(live_rows, lax.axis_index("own") * mats + core, 0, keepdims=False)
-    counts = [192, 240, height]
-    level = sum((live > rows).astype(jnp.int32) for rows in counts[:-1])
+    step, least = 16, 176
+    counts = range(least, height + 1, step)
+    level = jnp.maximum(live - least + step - 1, 0) // step
     mine = lax.switch(level, [functools.partial(chain, rows) for rows in counts])
     back = lax.all_gather(mine, "core")
     new_momentum, update = finish(

time: 62.7 us -> 69.6 us (1.11)
  blocking collectives: 40.8 us -> 48 us
    all_gather x1, blocking collectives: 9.96 us -> 17.7 us  [per_device(): back = lax.all_gather(mine, 'core')]
    all_to_all x1, blocking collectives: 11 us -> 9.18 us  [chain(): chunks = lax.all_to_all(chunks, group, 0, 0)]
    all_to_all x1, blocking collectives: 9.61 us -> 10.8 us  [chain(): gathered = lax.all_to_all(copies, group, 0, 0)]
  transfers between devices with their start and end apart: 1 -> 1, of which waited for: 0 -> 1; matrix products, arithmetic and copies ran while one was open for 1% -> 1% of each run, Pallas kernels for 0% -> 0%
where the time goes in v6:
time: 69.6 us; the launch traced here: 69.3 us
  blocking collectives  48 us (69%)
  starting transfers between devices  12.4 us (18%)
  Pallas kernels  6.3 us (9%)
  between operations  1.37 us (2%)
    all_gather x1, blocking collectives, per_device(): back = lax.all_gather(mine, 'core')  17.7 us
    ppermute x1, starting transfers between devices, per_device(): other = lax.ppermute(take_other(grads[0], old), 'core', [(0, 1), (1, 0)])  12.4 us
    all_to_all x1, blocking collectives, chain(): gathered = lax.all_to_all(copies, group, 0, 0)  10.8 us
    all_to_all x1, blocking collectives, chain(): chunk = lax.all_to_all(chunk, 'y_high', 0, 0)  10.3 us
    all_to_all x1, blocking collectives, chain(): chunks = lax.all_to_all(chunks, group, 0, 0)  9.18 us
    pallas_call x1, Pallas kernels, newton(): pl.pallas_call(newton_kernel, in_specs=[VMEM], out_specs=VMEM, out_shape=...  3.39 us
    pallas_call x1, Pallas kernels, take_other(): pl.pallas_call(take_kernel, in_specs=[VMEM, VMEM], out_specs=VMEM, out_sh...  1.69 us
  transfers between devices with their start and end apart: 1, of which 1 were waited for; matrix products, arithmetic and copies ran while one was open for 1% of the time, Pallas kernels for 0%

profile of v6, /device:TPU:1, one launch (start us, length us, event | category | flops | bytes accessed | tf_op | source)
XLA Modules:
  0.0 69.3 jit_solution(16845877690451331678)
XLA Ops:
  0.6 0.0 copy-start.1
  0.6 0.0 copy-start.2
  0.6 0.0 copy-start.3
  0.7 1.7 %shard_map.59 = bf16[288,1024]{1,0:T(8,128)(2,1)S(1)} custom-call(bf16[2,288,1024]{2,1,0:T(8,128)(2,1)} %bitcast.26, f32[2,16,288]{2,1,0:T(8,128)} %bitcast.35), custom_call_target="tpu_custom_call" | custom-call | tf_op jit(solution)/shard_map/pallas_call | solution.py:56
  2.4 12.4 %collective-permute-start = (bf16[288,1024]{1,0:T(8,128)(2,1)S(1)}, bf16[288,1024]{1,0:T(8,128)(2,1)S(1)}, u32[]{:S(2)}, u32[]{:S(2)}) collective-permute-start(bf16[288,1024]{1,0:T(8,128)(2,1)S(1)} %shard_map.59), channel_id=1, source_target_pairs={{0,12},{12,0},{1,13},{13,1},{2,14},{14,2},{3,15},{15,3},{4,16},{16... | collective-permute-start | bytes 1769480 | tf_op jit(solution)/shard_map/ppermute | solution.py:215
  14.8 0.0 copy-done.3
  14.8 0.6 dynamic_slice.4
  16.1 0.3 collective-permute-done
  16.4 0.0 copy-done.1
  16.4 0.0 copy-done.2
  16.4 0.0 copy-start
  16.4 34.5 %conditional.1 = (f32[2,32,288]{2,1,0:T(8,128)S(1)}) conditional(s32[]{:T(128)} %clamp.3, (s32[24]{0:T(128)S(1)}, bf16[1,2,288,1024]{3,2,1,0:T(8,128)(2,1)S(1)}, bf16[288,1024]{1,0:T(8,128)(2,1)S(1)}, f32[2,16,288]{2,1,0:T(8,128)S(1)}) %tuple.58, (s32[24]{0:T(128)S(1)}, bf16[1,2,288,1024]{3,2,1,0:T(8,128)(2,1)S(1)}, ...), branch_computations={%region_0.1_spmd, %region_1.2_spmd, %region_2.3_spmd, %region_3.4_... | conditional | bytes 2949128 | solution.py:229
  16.4 0.4 branch_0_fun.4
  16.8 9.2 %all_to_all.96.parts_ref = bf16[8,176,128]{2,1,0:T(8,128)(2,1)S(1)} all-to-all(bf16[8,176,128]{2,1,0:T(8,128)(2,1)S(1)} %branch_0_fun.4), channel_id=1, replica_groups=mesh['x'=4,'y_high'=4,'y_low'=2,'core'=2,'own'=12] {'x','y_low'}, dimensions={0} | all-to-all | bytes 720896 | tf_op jit(solution)/shard_map/cond/branch_0_fun/all_to_all | solution.py:218
  26.0 0.1 branch_0_fun.5
  26.0 10.3 %all_to_all.97.parts_ref = bf16[4,176,128]{2,1,0:T(8,128)(2,1)S(1)} all-to-all(bf16[4,176,128]{2,1,0:T(8,128)(2,1)S(1)} %branch_0_fun.5), channel_id=1, replica_groups=mesh['x'=4,'y_high'=4,'y_low'=2,'core'=2,'own'=12] {'y_high'}, dimensions={0} | all-to-all | bytes 360448 | tf_op jit(solution)/shard_map/cond/branch_0_fun/all_to_all | solution.py:220
  36.4 0.1 branch_0_fun.6
  36.5 10.8 %all_to_all.98.gathered_ref = bf16[8,176,128]{2,1,0:T(8,128)(2,1)S(1)} all-to-all(bf16[8,176,128]{2,1,0:T(8,128)(2,1)S(1)} %branch_0_fun.6), channel_id=1, replica_groups=mesh['x'=4,'y_high'=4,'y_low'=2,'core'=2,'own'=12] {'x','y_low'}, dimensions={0} | all-to-all | bytes 720896 | tf_op jit(solution)/shard_map/cond/branch_0_fun/all_to_all | solution.py:222
  47.3 3.4 %branch_0_fun.7 = f32[2,32,288]{2,1,0:T(8,128)S(1)} custom-call(bf16[8,176,128]{2,1,0:T(8,128)(2,1)S(1)} %all_to_all.98.gathered_ref), custom_call_target="tpu_custom_call" | custom-call | tf_op jit(solution)/shard_map/cond/branch_0_fun/pallas_call | solution.py:176
  51.0 17.7 %all-gather = f32[4,32,288]{2,1,0:T(8,128)S(1)} all-gather(f32[2,32,288]{2,1,0:T(8,128)S(1)} %get-tuple-element.111), channel_id=2, replica_groups=mesh['x'=4,'y_high'=4,'y_low'=2,'core'=2,'own'=12] {'core'}, dimensions={0}, use_global_device_ids=true | all-gather | bytes 221184 | tf_op jit(solution)/shard_map/all_gather | solution.py:230
  68.7 0.0 copy-done
  68.7 0.6 shard_map.60
Async XLA Ops:
  0.6 15.8 %copy-start.1 = (bf16[1,2,288,1024]{3,2,1,0:T(8,128)(2,1)S(1)}, bf16[1,2,288,1024]{3,2,1,0:T(8,128)(2,1)}, u32[]{:S(2)}) copy-start(bf16[1,2,288,1024]{3,2,1,0:T(8,128)(2,1)} %param.12) | copy-start | bytes 3538948
  0.6 15.8 %copy-start.2 = (f32[2,288,16]{1,2,0:T(8,128)S(1)}, f32[2,288,16]{1,2,0:T(8,128)}, u32[]{:S(2)}) copy-start(f32[2,288,16]{1,2,0:T(8,128)} %param.13) | copy-start | bytes 110596
  0.6 14.2 %copy-start.3 = (s32[24]{0:T(128)S(1)}, s32[24]{0:T(128)}, u32[]{:S(2)}) copy-start(s32[24]{0:T(128)} %param.15) | copy-start | bytes 292
  2.4 14.0 %collective-permute-start = (bf16[288,1024]{1,0:T(8,128)(2,1)S(1)}, bf16[288,1024]{1,0:T(8,128)(2,1)S(1)}, u32[]{:S(2)}, u32[]{:S(2)}) collective-permute-start(bf16[288,1024]{1,0:T(8,128)(2,1)S(1)} %shard_map.59), channel_id=1, source_target_pairs={{0,12},{12,0},{1,13},{13,1},{2,14},{14,2},{3,15},{15,3},{4,16},{16... | collective-permute-start | bytes 1769480 | tf_op jit(solution)/shard_map/ppermute | solution.py:215
  16.4 52.3 %copy-start = (f32[2,288,16]{1,2,0:T(8,128)S(1)}, f32[2,288,16]{1,2,0:T(8,128)}, u32[]{:S(2)}) copy-start(f32[2,288,16]{1,2,0:T(8,128)} %param.14) | copy-start | bytes 110596

commit v7 on v6

--- a/solution.py
+++ b/solution.py
@@ -223,7 +223,7 @@
         return newton(gathered, cores * slab, height)
 
     live = lax.dynamic_index_in_dim(live_rows, lax.axis_index("own") * mats + core, 0, keepdims=False)
-    step, least = 16, 176
+    step, least = 32, 192
     counts = range(least, height + 1, step)
     level = jnp.maximum(live - least + step - 1, 0) // step
     mine = lax.switch(level, [functools.partial(chain, rows) for rows in counts])

time: 69.6 us -> 59.6 us (0.86)
  blocking collectives: 48 us -> 37.6 us
    all_gather x1, blocking collectives: 17.7 us -> 7.25 us  [per_device(): back = lax.all_gather(mine, 'core')]
    all_to_all x1, blocking collectives: 9.18 us -> 10.7 us  [chain(): chunks = lax.all_to_all(chunks, group, 0, 0)]
    all_to_all x1, blocking collectives: 10.8 us -> 9.55 us  [chain(): gathered = lax.all_to_all(copies, group, 0, 0)]
where the time goes in v7:
time: 59.6 us; the launch traced here: 59 us
  blocking collectives  37.6 us (63%)
  starting transfers between devices  12.4 us (21%)
  Pallas kernels  6.5 us (11%)
  between operations  1.37 us (2%)
  local copies, waits for them, and re-layouts  0.6 us (1%)
    ppermute x1, starting transfers between devices, per_device(): other = lax.ppermute(take_other(grads[0], old), 'core', [(0, 1), (1, 0)])  12.4 us
    all_to_all x1, blocking collectives, chain(): chunks = lax.all_to_all(chunks, group, 0, 0)  10.7 us
    all_to_all x1, blocking collectives, chain(): chunk = lax.all_to_all(chunk, 'y_high', 0, 0)  10 us
    all_to_all x1, blocking collectives, chain(): gathered = lax.all_to_all(copies, group, 0, 0)  9.55 us
    all_gather x1, blocking collectives, per_device(): back = lax.all_gather(mine, 'core')  7.25 us
    pallas_call x1, Pallas kernels, newton(): pl.pallas_call(newton_kernel, in_specs=[VMEM], out_specs=VMEM, out_shape=...  3.56 us
    pallas_call x1, Pallas kernels, take_other(): pl.pallas_call(take_kernel, in_specs=[VMEM, VMEM], out_specs=VMEM, out_sh...  1.69 us
  transfers between devices with their start and end apart: 1, of which 1 were waited for; matrix products, arithmetic and copies ran while one was open for 1% of the time, Pallas kernels for 0%

profile of v7, /device:TPU:1, one launch (start us, length us, event | category | flops | bytes accessed | tf_op | source)
XLA Modules:
  0.0 59.0 jit_solution(10005401353837677762)
XLA Ops:
  0.6 0.0 copy-start.1
  0.6 0.0 copy-start.2
  0.6 0.0 copy-start.3
  0.7 1.7 %shard_map.59 = bf16[288,1024]{1,0:T(8,128)(2,1)S(1)} custom-call(bf16[2,288,1024]{2,1,0:T(8,128)(2,1)} %bitcast.18, f32[2,16,288]{2,1,0:T(8,128)} %bitcast.23), custom_call_target="tpu_custom_call" | custom-call | tf_op jit(solution)/shard_map/pallas_call | solution.py:56
  2.4 12.4 %collective-permute-start = (bf16[288,1024]{1,0:T(8,128)(2,1)S(1)}, bf16[288,1024]{1,0:T(8,128)(2,1)S(1)}, u32[]{:S(2)}, u32[]{:S(2)}) collective-permute-start(bf16[288,1024]{1,0:T(8,128)(2,1)S(1)} %shard_map.59), channel_id=1, source_target_pairs={{0,12},{12,0},{1,13},{13,1},{2,14},{14,2},{3,15},{15,3},{4,16},{16... | collective-permute-start | bytes 1769480 | tf_op jit(solution)/shard_map/ppermute | solution.py:215
  14.8 0.0 copy-done.3
  14.8 0.6 dynamic_slice.4
  16.1 0.3 collective-permute-done
  16.4 0.0 copy-done.1
  16.4 0.0 copy-done.2
  16.4 0.0 copy-start
  16.4 34.7 %conditional.1 = (f32[2,32,288]{2,1,0:T(8,128)S(1)}) conditional(s32[]{:T(128)} %clamp.3, (s32[24]{0:T(128)S(1)}, bf16[1,2,288,1024]{3,2,1,0:T(8,128)(2,1)S(1)}, bf16[288,1024]{1,0:T(8,128)(2,1)S(1)}, f32[2,16,288]{2,1,0:T(8,128)S(1)}) %tuple.34, (s32[24]{0:T(128)S(1)}, bf16[1,2,288,1024]{3,2,1,0:T(8,128)(2,1)S(1)}, ...), branch_computations={%region_0.1_spmd, %region_1.2_spmd, %region_2.3_spmd, %region_3.4_... | conditional | bytes 2949128 | solution.py:229
  16.4 0.4 branch_0_fun.4
  16.8 10.7 %all_to_all.48.parts_ref = bf16[8,192,128]{2,1,0:T(8,128)(2,1)S(1)} all-to-all(bf16[8,192,128]{2,1,0:T(8,128)(2,1)S(1)} %branch_0_fun.4), channel_id=1, replica_groups=mesh['x'=4,'y_high'=4,'y_low'=2,'core'=2,'own'=12] {'x','y_low'}, dimensions={0} | all-to-all | bytes 786432 | tf_op jit(solution)/shard_map/cond/branch_0_fun/all_to_all | solution.py:218
  27.6 0.1 branch_0_fun.5
  27.6 10.0 %all_to_all.49.parts_ref = bf16[4,192,128]{2,1,0:T(8,128)(2,1)S(1)} all-to-all(bf16[4,192,128]{2,1,0:T(8,128)(2,1)S(1)} %branch_0_fun.5), channel_id=1, replica_groups=mesh['x'=4,'y_high'=4,'y_low'=2,'core'=2,'own'=12] {'y_high'}, dimensions={0} | all-to-all | bytes 393216 | tf_op jit(solution)/shard_map/cond/branch_0_fun/all_to_all | solution.py:220
  37.7 0.1 branch_0_fun.6
  37.8 9.6 %all_to_all.50.gathered_ref = bf16[8,192,128]{2,1,0:T(8,128)(2,1)S(1)} all-to-all(bf16[8,192,128]{2,1,0:T(8,128)(2,1)S(1)} %branch_0_fun.6), channel_id=1, replica_groups=mesh['x'=4,'y_high'=4,'y_low'=2,'core'=2,'own'=12] {'x','y_low'}, dimensions={0} | all-to-all | bytes 786432 | tf_op jit(solution)/shard_map/cond/branch_0_fun/all_to_all | solution.py:222
  47.4 3.6 %branch_0_fun.7 = f32[2,32,288]{2,1,0:T(8,128)S(1)} custom-call(bf16[8,192,128]{2,1,0:T(8,128)(2,1)S(1)} %all_to_all.50.gathered_ref), custom_call_target="tpu_custom_call" | custom-call | tf_op jit(solution)/shard_map/cond/branch_0_fun/pallas_call | solution.py:176
  51.1 7.3 %all-gather = f32[4,32,288]{2,1,0:T(8,128)S(1)} all-gather(f32[2,32,288]{2,1,0:T(8,128)S(1)} %get-tuple-element.59), channel_id=2, replica_groups=mesh['x'=4,'y_high'=4,'y_low'=2,'core'=2,'own'=12] {'core'}, dimensions={0}, use_global_device_ids=true | all-gather | bytes 221184 | tf_op jit(solution)/shard_map/all_gather | solution.py:230
  58.3 0.0 copy-done
  58.3 0.6 %shard_map.60 = (f32[2,16,288]{2,1,0:T(8,128)}, f32[2,16,288]{2,1,0:T(8,128)}) custom-call(f32[2,2,32,288]{3,2,1,0:T(8,128)S(1)} %bitcast.16, f32[2,16,288]{2,1,0:T(8,128)S(1)} %bitcast.17), custom_call_target="tpu_custom_call" | custom-call | tf_op jit(solution)/shard_map/pallas_call | solution.py:199
Async XLA Ops:
  0.6 15.8 %copy-start.1 = (bf16[1,2,288,1024]{3,2,1,0:T(8,128)(2,1)S(1)}, bf16[1,2,288,1024]{3,2,1,0:T(8,128)(2,1)}, u32[]{:S(2)}) copy-start(bf16[1,2,288,1024]{3,2,1,0:T(8,128)(2,1)} %param.8) | copy-start | bytes 3538948
  0.6 15.8 %copy-start.2 = (f32[2,288,16]{1,2,0:T(8,128)S(1)}, f32[2,288,16]{1,2,0:T(8,128)}, u32[]{:S(2)}) copy-start(f32[2,288,16]{1,2,0:T(8,128)} %param.9) | copy-start | bytes 110596
  0.6 14.2 %copy-start.3 = (s32[24]{0:T(128)S(1)}, s32[24]{0:T(128)}, u32[]{:S(2)}) copy-start(s32[24]{0:T(128)} %param.11) | copy-start | bytes 292
  2.4 14.0 %collective-permute-start = (bf16[288,1024]{1,0:T(8,128)(2,1)S(1)}, bf16[288,1024]{1,0:T(8,128)(2,1)S(1)}, u32[]{:S(2)}, u32[]{:S(2)}) collective-permute-start(bf16[288,1024]{1,0:T(8,128)(2,1)S(1)} %shard_map.59), channel_id=1, source_target_pairs={{0,12},{12,0},{1,13},{13,1},{2,14},{14,2},{3,15},{15,3},{4,16},{16... | collective-permute-start | bytes 1769480 | tf_op jit(solution)/shard_map/ppermute | solution.py:215
  16.4 41.9 %copy-start = (f32[2,288,16]{1,2,0:T(8,128)S(1)}, f32[2,288,16]{1,2,0:T(8,128)}, u32[]{:S(2)}) copy-start(f32[2,288,16]{1,2,0:T(8,128)} %param.10) | copy-start | bytes 110596

commit v8 on v7

--- a/solution.py
+++ b/solution.py
@@ -31,6 +31,18 @@
 
 def mm(a, b, dims, precision=None):
     return lax.dot_general(a, b, dims, precision=precision, preferred_element_type=jnp.float32)
+
+
+def live_pair(live_ref):
+    first = lax.axis_index("own") * 2
+    ids = lax.broadcasted_iota(jnp.int32, live_ref.shape, 1)
+    rows = [jnp.where(ids == first + m, live_ref[...], 0) for m in range(2)]
+    return [jnp.sum(r, axis=1, keepdims=True) for r in rows]
+
+
+def swapped(live_ref):
+    low, high = live_pair(live_ref)
+    return (low > high).astype(jnp.int32)[0, 0]
 
 
 def spread_old(old):
@@ -45,45 +57,45 @@
     return mm(MOMENTUM_DECAY * old, pick, TN, lax.Precision.HIGHEST), chunk, lanes
 
 
-def take_kernel(grads_ref, old_ref, out_ref):
-    other = 1 - lax.axis_index("core")
+def take_kernel(live_ref, grads_ref, old_ref, out_ref):
+    other = (lax.axis_index("core") + 1 + swapped(live_ref)) % 2
     out_ref[...] = grads_ref[other]
     spread, _, lanes = spread_old(old_ref[other])
     out_ref[:, lanes] = (grads_ref[other, :, lanes].astype(jnp.float32) + spread).astype(jnp.bfloat16)
 
 
-def take_other(grads, old):
+def take_other(live, grads, old):
     return pl.pallas_call(
         take_kernel,
-        in_specs=[VMEM, VMEM],
+        in_specs=[VMEM, VMEM, VMEM],
         out_specs=VMEM,
         out_shape=jax.ShapeDtypeStruct(grads.shape[1:], grads.dtype),
         compiler_params=PARAMS,
-    )(grads, old)
-
-
-def pair_sum_kernel(own_ref, other_ref, old_ref, out_ref):
-    core = lax.axis_index("core")
+    )(live, grads, old)
+
+
+def pair_sum_kernel(live_ref, own_ref, other_ref, old_ref, out_ref):
+    held = (lax.axis_index("core") + swapped(live_ref)) % 2
     rows = out_ref.shape[1]
 
     def total(lanes):
-        return own_ref[core, :rows, lanes].astype(jnp.float32) + other_ref[:rows, lanes].astype(jnp.float32)
+        return own_ref[held, :rows, lanes].astype(jnp.float32) + other_ref[:rows, lanes].astype(jnp.float32)
 
     for q in range(out_ref.shape[0]):
         out_ref[q] = total(slice(q * LANES, (q + 1) * LANES)).astype(jnp.bfloat16)
-    spread, chunk, lanes = spread_old(old_ref[core])
+    spread, chunk, lanes = spread_old(old_ref[held])
     out_ref[chunk] = (total(lanes) + spread[:rows]).astype(jnp.bfloat16)
 
 
-def pair_sum(own, other, old, rows):
+def pair_sum(live, own, other, old, rows):
     width = other.shape[1]
     return pl.pallas_call(
         pair_sum_kernel,
-        in_specs=[VMEM, VMEM, VMEM],
+        in_specs=[VMEM, VMEM, VMEM, VMEM],
         out_specs=VMEM,
         out_shape=jax.ShapeDtypeStruct((width // LANES, rows, LANES), jnp.bfloat16),
         compiler_params=PARAMS,
-    )(own, other, old)
+    )(live, own, other, old)
 
 
 def add_parts(parts_ref):
@@ -109,25 +121,24 @@
     )(parts)
 
 
-def mask_kernel(mats, live_ref, parts_ref, copies_ref):
+def mask_kernel(live_ref, parts_ref, copies_ref):
     total = add_parts(parts_ref)
     rows = lax.broadcasted_iota(jnp.int32, total.shape, 0)
-    matrix = lax.axis_index("own") * mats + lax.axis_index("core")
-    which = lax.broadcasted_iota(jnp.int32, live_ref.shape, 1) == matrix
-    live = jnp.sum(jnp.where(which, live_ref[...], 0), axis=1, keepdims=True)
+    low, high = live_pair(live_ref)
+    live = jnp.where(lax.axis_index("core") == 0, jnp.minimum(low, high), jnp.maximum(low, high))
     new = jnp.where(rows < live, total, 0.0).astype(jnp.bfloat16)
     for k in range(copies_ref.shape[0]):
         copies_ref[k] = new
 
 
-def sum_mask_and_copy(mats, live_rows, parts, copies):
-    return pl.pallas_call(
-        functools.partial(mask_kernel, mats),
+def sum_mask_and_copy(live, parts, copies):
+    return pl.pallas_call(
+        mask_kernel,
         in_specs=[VMEM, VMEM],
         out_specs=VMEM,
         out_shape=jax.ShapeDtypeStruct((copies,) + parts.shape[1:], jnp.bfloat16),
         compiler_params=PARAMS,
-    )(live_rows[None, :], parts)
+    )(live, parts)
 
 
 def newton_kernel(gathered_ref, out_ref, x_ref):
@@ -183,26 +194,28 @@
     )(gathered)
 
 
-def finish_kernel(factor, back_ref, weights_ref, new_ref, update_ref):
+def finish_kernel(factor, live_ref, back_ref, weights_ref, new_ref, update_ref):
+    swap = swapped(live_ref)
     mats, slab, _ = weights_ref.shape
     mine = pl.ds(pl.multiple_of(lax.axis_index("core") * slab, slab), slab)
     for m in range(mats):
-        new_ref[m] = back_ref[m, 0, mine, :]
-        update_ref[m] = factor * back_ref[m, 1, mine, :] + WEIGHT_DECAY * weights_ref[m]
-
-
-def finish(back, weights, factor):
+        holder = (m + swap) % 2
+        new_ref[m] = back_ref[holder, 0, mine, :]
+        update_ref[m] = factor * back_ref[holder, 1, mine, :] + WEIGHT_DECAY * weights_ref[m]
+
+
+def finish(live, back, weights, factor):
     def kernel(*refs):
         finish_kernel(factor, *refs)
 
     shape = jax.ShapeDtypeStruct(weights.shape, jnp.float32)
     return pl.pallas_call(
         kernel,
-        in_specs=[VMEM, VMEM],
+        in_specs=[VMEM, VMEM, VMEM],
         out_specs=[VMEM, VMEM],
         out_shape=[shape, shape],
         compiler_params=PARAMS,
-    )(back, weights)
+    )(live, back, weights)
 
 
 def per_device(grads, momentum, weights, live_rows):
@@ -211,25 +224,27 @@
     width = grads.shape[3]
     core = lax.axis_index("core")
     group = ("x", "y_low")
+    live = live_rows[None, :]
     old = jnp.swapaxes(momentum, 1, 2)
-    other = lax.ppermute(take_other(grads[0], old), "core", [(0, 1), (1, 0)])
+    other = lax.ppermute(take_other(live, grads[0], old), "core", [(0, 1), (1, 0)])
     def chain(rows):
-        chunks = pair_sum(grads[0], other, old, rows)
+        chunks = pair_sum(live, grads[0], other, old, rows)
         chunks = lax.all_to_all(chunks, group, 0, 0)
         chunk = sum_and_copy(chunks, lax.axis_size("y_high"))
         chunk = lax.all_to_all(chunk, "y_high", 0, 0)
-        copies = sum_mask_and_copy(mats, live_rows, chunk, width // LANES)
+        copies = sum_mask_and_copy(live, chunk, width // LANES)
         gathered = lax.all_to_all(copies, group, 0, 0)
         return newton(gathered, cores * slab, height)
 
-    live = lax.dynamic_index_in_dim(live_rows, lax.axis_index("own") * mats + core, 0, keepdims=False)
+    pair = lax.dynamic_slice_in_dim(live_rows, lax.axis_index("own") * mats, mats)
+    held = jnp.where(core == 0, jnp.min(pair), jnp.max(pair))
     step, least = 32, 192
     counts = range(least, height + 1, step)
-    level = jnp.maximum(live - least + step - 1, 0) // step
+    level = jnp.maximum(held - least + step - 1, 0) // step
     mine = lax.switch(level, [functools.partial(chain, rows) for rows in counts])
     back = lax.all_gather(mine, "core")
     new_momentum, update = finish(
-        back, jnp.swapaxes(weights, 1, 2), UPDATE_SCALE * math.sqrt(width)
+        live, back, jnp.swapaxes(weights, 1, 2), UPDATE_SCALE * math.sqrt(width)
     )
     return (jnp.swapaxes(new_momentum, 1, 2), jnp.swapaxes(update, 1, 2))
 

time: 59.6 us -> 66.4 us (1.11)
  blocking collectives: 37.6 us -> 42.3 us
  Pallas kernels: 6.5 us -> 8.39 us
  other arithmetic: 0 us -> 0.71 us
  between operations: 1.37 us -> 2.05 us
    all_to_all x1, blocking collectives: 10.7 us -> 13.3 us  [chain(): chunks = lax.all_to_all(chunks, group, 0, 0)]
    all_to_all x1, blocking collectives: 10 us -> 12.5 us  [chain(): chunk = lax.all_to_all(chunk, 'y_high', 0, 0)]
    all_gather x1, blocking collectives: 7.25 us -> 5.43 us  [per_device(): back = lax.all_gather(mine, 'core')]
    all_to_all x1, blocking collectives: 9.55 us -> 11.1 us  [chain(): gathered = lax.all_to_all(copies, group, 0, 0)]
    pallas_call x1, Pallas kernels: 3.56 us -> 4.96 us  [newton(): pl.pallas_call(newton_kernel, in_specs=[VMEM], out_specs=VMEM, out_shape=...]
    reduce_max x0 -> x1, other arithmetic: none -> 0.71 us  [per_device(): held = jnp.where(core == 0, jnp.min(pair), jnp.max(pair))]
  transfers between devices with their start and end apart: 1 -> 1, of which waited for: 1 -> 0; matrix products, arithmetic and copies ran while one was open for 1% -> 1% of each run, Pallas kernels for 0% -> 0%
where the time goes in v8:
time: 66.4 us; the launch traced here: 66.1 us
  blocking collectives  42.3 us (64%)
  starting transfers between devices  12.4 us (19%)
  Pallas kernels  8.39 us (13%)
  between operations  2.05 us (3%)
  other arithmetic  0.71 us (1%)
    all_to_all x1, blocking collectives, chain(): chunks = lax.all_to_all(chunks, group, 0, 0)  13.3 us
    all_to_all x1, blocking collectives, chain(): chunk = lax.all_to_all(chunk, 'y_high', 0, 0)  12.5 us
    ppermute x1, starting transfers between devices, per_device(): lax.ppermute(take_other(live, grads[0], old), 'core', [(0, 1), (1, 0)])  12.4 us
    all_to_all x1, blocking collectives, chain(): gathered = lax.all_to_all(copies, group, 0, 0)  11.1 us
    all_gather x1, blocking collectives, per_device(): back = lax.all_gather(mine, 'core')  5.43 us
    pallas_call x1, Pallas kernels, newton(): pl.pallas_call(newton_kernel, in_specs=[VMEM], out_specs=VMEM, out_shape=...  4.96 us
    pallas_call x1, Pallas kernels, take_other(): pl.pallas_call(take_kernel, in_specs=[VMEM, VMEM, VMEM], out_specs=VMEM,...  1.85 us
  transfers between devices with their start and end apart: 1, of which 0 were waited for; matrix products, arithmetic and copies ran while one was open for 1% of the time, Pallas kernels for 0%

profile of v8, /device:TPU:1, one launch (start us, length us, event | category | flops | bytes accessed | tf_op | source)
XLA Modules:
  0.0 66.1 jit_solution(3854300358948775480)
XLA Ops:
  0.6 0.0 copy-start.3
  0.6 0.0 copy-start.1
  0.6 0.0 copy-start.2
  0.7 1.8 %shard_map.59 = bf16[288,1024]{1,0:T(8,128)(2,1)S(1)} custom-call(s32[1,24]{1,0:T(1,128)} %bitcast.23, bf16[2,288,1024]{2,1,0:T(8,128)(2,1)} %bitcast.13, f32[2,16,288]{2,1,0:T(8,128)} %bitcast.18), custom_call_target="tpu_custom_call" | custom-call | tf_op jit(solution)/shard_map/pallas_call | solution.py:68
  2.5 12.4 %collective-permute-start = (bf16[288,1024]{1,0:T(8,128)(2,1)S(1)}, bf16[288,1024]{1,0:T(8,128)(2,1)S(1)}, u32[]{:S(2)}, u32[]{:S(2)}) collective-permute-start(bf16[288,1024]{1,0:T(8,128)(2,1)S(1)} %shard_map.59), channel_id=1, source_target_pairs={{0,12},{12,0},{1,13},{13,1},{2,14},{14,2},{3,15},{15,3},{4,16},{16... | collective-permute-start | bytes 1769480 | tf_op jit(solution)/shard_map/ppermute | solution.py:229
  15.0 0.0 copy-done.3
  15.0 0.7 %dynamic-slice_reduce_fusion = (s32[]{:T(128)}, s32[]{:T(128)}) fusion(s32[24]{0:T(128)S(1)} %copy-done.3, s32[]{:T(128)S(6)} %select_n.11), kind=kLoop, calls=%fused_computation | loop fusion | flops 2 | bytes 20 | tf_op jit(solution)/shard_map/reduce_max | solution.py:240
  17.0 0.0 collective-permute-done
  17.0 0.0 copy-done.1
  17.0 0.0 copy-done.2
  17.0 0.0 copy-start
  17.0 42.9 %conditional.1 = (f32[2,32,288]{2,1,0:T(8,128)S(1)}) conditional(s32[]{:T(128)} %clamp.3, (bf16[1,2,288,1024]{3,2,1,0:T(8,128)(2,1)S(1)}, s32[1,24]{1,0:T(1,128)S(1)}, bf16[288,1024]{1,0:T(8,128)(2,1)S(1)}, f32[2,16,288]{2,1,0:T(8,128)S(1)}) %tuple.35, (bf16[1,2,288,1024]{3,2,1,0:T(8,128)(2,1)S(1)}, ...), branch_computations={%region_2.3_spmd, %region_3.4_spmd, %region_4.5_spmd, %region_5.6_... | conditional | bytes 2949128 | solution.py:244
  17.1 0.6 branch_3_fun.4
  17.7 13.3 %all_to_all.57.parts_ref = bf16[8,288,128]{2,1,0:T(8,128)(2,1)S(1)} all-to-all(bf16[8,288,128]{2,1,0:T(8,128)(2,1)S(1)} %branch_3_fun.4), channel_id=1, replica_groups=mesh['x'=4,'y_high'=4,'y_low'=2,'core'=2,'own'=12] {'x','y_low'}, dimensions={0} | all-to-all | bytes 1179648 | tf_op jit(solution)/shard_map/cond/branch_3_fun/all_to_all | solution.py:232
  31.0 0.1 branch_3_fun.5
  31.1 12.5 %all_to_all.58.parts_ref = bf16[4,288,128]{2,1,0:T(8,128)(2,1)S(1)} all-to-all(bf16[4,288,128]{2,1,0:T(8,128)(2,1)S(1)} %branch_3_fun.5), channel_id=1, replica_groups=mesh['x'=4,'y_high'=4,'y_low'=2,'core'=2,'own'=12] {'y_high'}, dimensions={0} | all-to-all | bytes 589824 | tf_op jit(solution)/shard_map/cond/branch_3_fun/all_to_all | solution.py:234
  43.5 0.1 branch_3_fun.6
  43.7 11.1 %all_to_all.59.gathered_ref = bf16[8,288,128]{2,1,0:T(8,128)(2,1)S(1)} all-to-all(bf16[8,288,128]{2,1,0:T(8,128)(2,1)S(1)} %branch_3_fun.6), channel_id=1, replica_groups=mesh['x'=4,'y_high'=4,'y_low'=2,'core'=2,'own'=12] {'x','y_low'}, dimensions={0} | all-to-all | bytes 1179648 | tf_op jit(solution)/shard_map/cond/branch_3_fun/all_to_all | solution.py:236
  54.7 5.0 %branch_3_fun.7 = f32[2,32,288]{2,1,0:T(8,128)S(1)} custom-call(bf16[8,288,128]{2,1,0:T(8,128)(2,1)S(1)} %all_to_all.59.gathered_ref), custom_call_target="tpu_custom_call" | custom-call | tf_op jit(solution)/shard_map/cond/branch_3_fun/pallas_call | solution.py:187
  59.9 5.4 %all-gather = f32[4,32,288]{2,1,0:T(8,128)S(1)} all-gather(f32[2,32,288]{2,1,0:T(8,128)S(1)} %get-tuple-element.61), channel_id=2, replica_groups=mesh['x'=4,'y_high'=4,'y_low'=2,'core'=2,'own'=12] {'core'}, dimensions={0}, use_global_device_ids=true | all-gather | bytes 221184 | tf_op jit(solution)/shard_map/all_gather | solution.py:245
  65.4 0.0 copy-done
  65.4 0.8 %shard_map.60 = (f32[2,16,288]{2,1,0:T(8,128)}, f32[2,16,288]{2,1,0:T(8,128)}) custom-call(s32[1,24]{1,0:T(1,128)S(1)} %bitcast.28, f32[2,2,32,288]{3,2,1,0:T(8,128)S(1)} %bitcast.11, f32[2,16,288]{2,1,0:T(8,128)S(1)} %bitcast.12), custom_call_target="tpu_custom_call" | custom-call | tf_op jit(solution)/shard_map/pallas_call | solution.py:212
Async XLA Ops:
  0.6 14.3 %copy-start.3 = (s32[24]{0:T(128)S(1)}, s32[24]{0:T(128)}, u32[]{:S(2)}) copy-start(s32[24]{0:T(128)} %param.11) | copy-start | bytes 292
  0.6 16.4 %copy-start.1 = (bf16[1,2,288,1024]{3,2,1,0:T(8,128)(2,1)S(1)}, bf16[1,2,288,1024]{3,2,1,0:T(8,128)(2,1)}, u32[]{:S(2)}) copy-start(bf16[1,2,288,1024]{3,2,1,0:T(8,128)(2,1)} %param.8) | copy-start | bytes 3538948
  0.6 16.4 %copy-start.2 = (f32[2,288,16]{1,2,0:T(8,128)S(1)}, f32[2,288,16]{1,2,0:T(8,128)}, u32[]{:S(2)}) copy-start(f32[2,288,16]{1,2,0:T(8,128)} %param.9) | copy-start | bytes 110596
  2.5 14.5 %collective-permute-start = (bf16[288,1024]{1,0:T(8,128)(2,1)S(1)}, bf16[288,1024]{1,0:T(8,128)(2,1)S(1)}, u32[]{:S(2)}, u32[]{:S(2)}) collective-permute-start(bf16[288,1024]{1,0:T(8,128)(2,1)S(1)} %shard_map.59), channel_id=1, source_target_pairs={{0,12},{12,0},{1,13},{13,1},{2,14},{14,2},{3,15},{15,3},{4,16},{16... | collective-permute-start | bytes 1769480 | tf_op jit(solution)/shard_map/ppermute | solution.py:229
  17.0 48.3 %copy-start = (f32[2,288,16]{1,2,0:T(8,128)S(1)}, f32[2,288,16]{1,2,0:T(8,128)}, u32[]{:S(2)}) copy-start(f32[2,288,16]{1,2,0:T(8,128)} %param.10) | copy-start | bytes 110596

commit v9 on v7

--- a/solution.py
+++ b/solution.py
@@ -223,7 +223,7 @@
         return newton(gathered, cores * slab, height)
 
     live = lax.dynamic_index_in_dim(live_rows, lax.axis_index("own") * mats + core, 0, keepdims=False)
-    step, least = 32, 192
+    step, least = 16, 192
     counts = range(least, height + 1, step)
     level = jnp.maximum(live - least + step - 1, 0) // step
     mine = lax.switch(level, [functools.partial(chain, rows) for rows in counts])

time: 59.6 us -> 67.2 us (1.13)
  the two profiles are of different devices: /device:TPU:1 before, /device:TPU:449 now
where the time goes in v9:
time: 67.2 us; the launch traced here: 66.9 us
  blocking collectives  47.4 us (71%)
  Pallas kernels  8.04 us (12%)
  loops' own time  6.53 us (10%)
  starting transfers between devices  2.58 us (4%)
  between operations  1.37 us (2%)
    all_to_all x1, blocking collectives, chain(): chunks = lax.all_to_all(chunks, group, 0, 0)  15 us
    all_to_all x1, blocking collectives, chain(): chunk = lax.all_to_all(chunk, 'y_high', 0, 0)  14.6 us
    all_to_all x1, blocking collectives, chain(): gathered = lax.all_to_all(copies, group, 0, 0)  13.2 us
    another operation x1, loops' own time, per_device(): lax.switch(level, [functools.partial(chain, rows) for rows in counts])  6.53 us
    pallas_call x1, Pallas kernels, newton(): pl.pallas_call(newton_kernel, in_specs=[VMEM], out_specs=VMEM, out_shape=...  4.95 us
    all_gather x1, blocking collectives, per_device(): back = lax.all_gather(mine, 'core')  4.59 us
    ppermute x1, starting transfers between devices, per_device(): other = lax.ppermute(take_other(grads[0], old), 'core', [(0, 1), (1, 0)])  2.58 us
    pallas_call x1, Pallas kernels, take_other(): pl.pallas_call(take_kernel, in_specs=[VMEM, VMEM], out_specs=VMEM, out_sh...  1.69 us
  transfers between devices with their start and end apart: 1, of which 1 were waited for; matrix products, arithmetic and copies ran while one was open for 1% of the time, Pallas kernels for 0%

profile of v9, /device:TPU:449, one launch (start us, length us, event | category | flops | bytes accessed | tf_op | source)
XLA Modules:
  0.0 66.9 jit_solution(2933350561130552325)
XLA Ops:
  0.6 0.0 copy-start.1
  0.6 0.0 copy-start.2
  0.6 0.0 copy-start.3
  0.7 1.7 %shard_map.59 = bf16[288,1024]{1,0:T(8,128)(2,1)S(1)} custom-call(bf16[2,288,1024]{2,1,0:T(8,128)(2,1)} %bitcast.24, f32[2,16,288]{2,1,0:T(8,128)} %bitcast.32), custom_call_target="tpu_custom_call" | custom-call | tf_op jit(solution)/shard_map/pallas_call | solution.py:56
  2.4 2.6 %collective-permute-start = (bf16[288,1024]{1,0:T(8,128)(2,1)S(1)}, bf16[288,1024]{1,0:T(8,128)(2,1)S(1)}, u32[]{:S(2)}, u32[]{:S(2)}) collective-permute-start(bf16[288,1024]{1,0:T(8,128)(2,1)S(1)} %shard_map.59), channel_id=1, source_target_pairs={{0,12},{12,0},{1,13},{13,1},{2,14},{14,2},{3,15},{15,3},{4,16},{16... | collective-permute-start | bytes 1769480 | tf_op jit(solution)/shard_map/ppermute | solution.py:215
  5.0 0.0 copy-done.3
  5.0 0.6 dynamic_slice.4
  6.2 0.3 collective-permute-done
  6.6 0.0 copy-done.1
  6.6 0.0 copy-done.2
  6.6 0.0 copy-start
  6.6 55.1 %conditional.1 = (f32[2,32,288]{2,1,0:T(8,128)S(1)}) conditional(s32[]{:T(128)} %clamp.3, (s32[24]{0:T(128)S(1)}, bf16[1,2,288,1024]{3,2,1,0:T(8,128)(2,1)S(1)}, bf16[288,1024]{1,0:T(8,128)(2,1)S(1)}, f32[2,16,288]{2,1,0:T(8,128)S(1)}) %tuple.52, (s32[24]{0:T(128)S(1)}, bf16[1,2,288,1024]{3,2,1,0:T(8,128)(2,1)S(1)}, ...), branch_computations={%region_0.1_spmd, %region_1.2_spmd, %region_2.3_spmd, %region_3.4_... | conditional | bytes 2949128 | solution.py:229
  12.9 0.5 branch_6_fun.4
  13.4 15.0 %all_to_all.102.parts_ref = bf16[8,288,128]{2,1,0:T(8,128)(2,1)S(1)} all-to-all(bf16[8,288,128]{2,1,0:T(8,128)(2,1)S(1)} %branch_6_fun.4), channel_id=1, replica_groups=mesh['x'=4,'y_high'=4,'y_low'=2,'core'=2,'own'=12] {'x','y_low'}, dimensions={0} | all-to-all | bytes 1179648 | tf_op jit(solution)/shard_map/cond/branch_6_fun/all_to_all | solution.py:218
  28.4 0.1 branch_6_fun.5
  28.5 14.6 %all_to_all.103.parts_ref = bf16[4,288,128]{2,1,0:T(8,128)(2,1)S(1)} all-to-all(bf16[4,288,128]{2,1,0:T(8,128)(2,1)S(1)} %branch_6_fun.5), channel_id=1, replica_groups=mesh['x'=4,'y_high'=4,'y_low'=2,'core'=2,'own'=12] {'y_high'}, dimensions={0} | all-to-all | bytes 589824 | tf_op jit(solution)/shard_map/cond/branch_6_fun/all_to_all | solution.py:220
  43.1 0.1 branch_6_fun.6
  43.2 13.2 %all_to_all.104.gathered_ref = bf16[8,288,128]{2,1,0:T(8,128)(2,1)S(1)} all-to-all(bf16[8,288,128]{2,1,0:T(8,128)(2,1)S(1)} %branch_6_fun.6), channel_id=1, replica_groups=mesh['x'=4,'y_high'=4,'y_low'=2,'core'=2,'own'=12] {'x','y_low'}, dimensions={0} | all-to-all | bytes 1179648 | tf_op jit(solution)/shard_map/cond/branch_6_fun/all_to_all | solution.py:222
  56.4 5.0 %branch_6_fun.7 = f32[2,32,288]{2,1,0:T(8,128)S(1)} custom-call(bf16[8,288,128]{2,1,0:T(8,128)(2,1)S(1)} %all_to_all.104.gathered_ref), custom_call_target="tpu_custom_call" | custom-call | tf_op jit(solution)/shard_map/cond/branch_6_fun/pallas_call | solution.py:176
  61.6 4.6 %all-gather = f32[4,32,288]{2,1,0:T(8,128)S(1)} all-gather(f32[2,32,288]{2,1,0:T(8,128)S(1)} %get-tuple-element.98), channel_id=2, replica_groups=mesh['x'=4,'y_high'=4,'y_low'=2,'core'=2,'own'=12] {'core'}, dimensions={0}, use_global_device_ids=true | all-gather | bytes 221184 | tf_op jit(solution)/shard_map/all_gather | solution.py:230
  66.2 0.0 copy-done
  66.2 0.6 shard_map.60
Async XLA Ops:
  0.6 5.9 %copy-start.1 = (bf16[1,2,288,1024]{3,2,1,0:T(8,128)(2,1)S(1)}, bf16[1,2,288,1024]{3,2,1,0:T(8,128)(2,1)}, u32[]{:S(2)}) copy-start(bf16[1,2,288,1024]{3,2,1,0:T(8,128)(2,1)} %param.11) | copy-start | bytes 3538948
  0.6 5.9 %copy-start.2 = (f32[2,288,16]{1,2,0:T(8,128)S(1)}, f32[2,288,16]{1,2,0:T(8,128)}, u32[]{:S(2)}) copy-start(f32[2,288,16]{1,2,0:T(8,128)} %param.12) | copy-start | bytes 110596
  0.6 4.3 %copy-start.3 = (s32[24]{0:T(128)S(1)}, s32[24]{0:T(128)}, u32[]{:S(2)}) copy-start(s32[24]{0:T(128)} %param.14) | copy-start | bytes 292
  2.4 4.2 %collective-permute-start = (bf16[288,1024]{1,0:T(8,128)(2,1)S(1)}, bf16[288,1024]{1,0:T(8,128)(2,1)S(1)}, u32[]{:S(2)}, u32[]{:S(2)}) collective-permute-start(bf16[288,1024]{1,0:T(8,128)(2,1)S(1)} %shard_map.59), channel_id=1, source_target_pairs={{0,12},{12,0},{1,13},{13,1},{2,14},{14,2},{3,15},{15,3},{4,16},{16... | collective-permute-start | bytes 1769480 | tf_op jit(solution)/shard_map/ppermute | solution.py:215
  6.6 59.7 %copy-start = (f32[2,288,16]{1,2,0:T(8,128)S(1)}, f32[2,288,16]{1,2,0:T(8,128)}, u32[]{:S(2)}) copy-start(f32[2,288,16]{1,2,0:T(8,128)} %param.13) | copy-start | bytes 110596
